TPU v7x, 256 devices: a whole 4x4x8 slice. The times are simulated.
256 devices in a mesh: gx: 64 (over z, y, core), gy: 4 (over x).
Axes of the slice: x: 4, y: 4, z: 8, core: 2. Of those that a mesh axis runs over, the one named last changes fastest.
Arguments:
- pressure: float32 [1024, 256, 128], P('gx', 'gy'), may hold values from -6 to 6
- inverse_density: float32 [1024, 256, 128], P('gx', 'gy'), may hold values from 0.04 to 2
- source: float32 [1024, 256, 128], P('gx', 'gy'), may hold values from -6 to 6
Outputs:
- updated_pressure: float32 [1024, 256, 128], P('gx', 'gy')
- residual: float32 [1024, 256, 128], P('gx', 'gy')
All inputs are finite; a program needn't handle non-finite values.
Results may differ from a plain program's by a relative error of at most 0.0003.
Values sent between devices are 32-bit elements; how exact they have to be, the bound alone decides.
A program may use at most 192 MiB of HBM per device.

v0:
```python
import jax
import jax.numpy as jnp
from jax import lax
from jax.sharding import PartitionSpec as P

LEVELS = 4
PRE = 2
POST = 2
COARSE = 8


OMEGA = 0.8


def with_halo(block, sides, width):
    for axis, dim in sides:
        count = lax.axis_size(axis)
        forward = [(i, i + 1) for i in range(count - 1)]
        forward.append((count - 1, 0))
        backward = [(target, source) for source, target in forward]
        low = lax.ppermute(
            lax.slice_in_dim(block, block.shape[dim] - width, None, axis=dim), axis, forward
        )
        high = lax.ppermute(lax.slice_in_dim(block, 0, width, axis=dim), axis, backward)
        block = jnp.concatenate([low, block, high], axis=dim)
    return block


def neighbor_terms(padded_press, padded_coef, factor):
    centre = padded_press[1:-1, 1:-1]
    centre_k = padded_coef[1:-1, 1:-1]
    neighbours = [
        (padded_press[2:, 1:-1], padded_coef[2:, 1:-1]),
        (padded_press[:-2, 1:-1], padded_coef[:-2, 1:-1]),
        (padded_press[1:-1, 2:], padded_coef[1:-1, 2:]),
        (padded_press[1:-1, :-2], padded_coef[1:-1, :-2]),
        (jnp.roll(centre, -1, 2), jnp.roll(centre_k, -1, 2)),
        (jnp.roll(centre, 1, 2), jnp.roll(centre_k, 1, 2)),
    ]
    fluxes = jnp.zeros_like(centre)
    totals = jnp.zeros_like(centre)
    for near_press, near_coef in neighbours:
        face_coef = 2.0 * centre_k * near_coef / (centre_k + near_coef)
        totals = totals + face_coef
        fluxes = fluxes + face_coef * (centre - near_press)
    return (factor * fluxes, factor * totals)


def relax(padded_press, padded_coef, source_part, factor):
    applied, diagonal = neighbor_terms(padded_press, padded_coef, factor)
    return padded_press[1:-1, 1:-1] + OMEGA * (source_part - applied) / diagonal


def coarsen(field):
    sx, sy, sz = field.shape
    return field.reshape(sx // 2, 2, sy // 2, 2, sz // 2, 2).mean(axis=(1, 3, 5))


def refine(field):
    return jnp.repeat(jnp.repeat(jnp.repeat(field, 2, 0), 2, 1), 2, 2)


def halo_press(field):
    return with_halo(field, (("gx", 0), ("gy", 1)), 1)


def level_context(coef):
    return with_halo(coef, (("gx", 0), ("gy", 1)), 1)


def smooth(current, padded_coef, target, factor, sweeps):
    for sweep_index in range(sweeps):
        current = relax(halo_press(current), padded_coef, target, factor)
    return current


def per_device(pressure, inverse_density, source):
    coefficients = [inverse_density]
    for level_index in range(LEVELS):
        coefficients.append(coarsen(coefficients[-1]))
    spread_levels = LEVELS
    current = pressure
    target = source
    saved_levels = []
    for level_index in range(spread_levels):
        factor = 0.25**level_index
        padded_coef = level_context(coefficients[level_index])
        current = smooth(current, padded_coef, target, factor, PRE)
        applied, unused = neighbor_terms(halo_press(current), padded_coef, factor)
        saved_levels.append((current, target, padded_coef))
        target = coarsen(target - applied)
        current = jnp.zeros_like(target)
    factor = 0.25**LEVELS
    padded_coef = level_context(coefficients[LEVELS])
    current = smooth(current, padded_coef, target, factor, COARSE)
    for level_index in reversed(range(spread_levels)):
        factor = 0.25**level_index
        below, target, padded_coef = saved_levels[level_index]
        current = below + refine(current)
        current = smooth(current, padded_coef, target, factor, POST)
    applied, unused = neighbor_terms(halo_press(current), saved_levels[0][2], 1.0)
    return (current, source - applied)


def solution(mesh):
    in_specs = (P("gx", "gy", None), P("gx", "gy", None), P("gx", "gy", None))
    out_specs = (P("gx", "gy", None), P("gx", "gy", None))
    return jax.shard_map(
        per_device, mesh=mesh, in_specs=in_specs, out_specs=out_specs, check_vma=False
    )
```

profile of v0, /device:TPU:2, one launch (start us, length us, event | category | flops | bytes accessed | tf_op | source)
XLA Modules:
  0.0 673.8 jit_solution(17928555265781319951)
XLA Ops:
  1.2 7.7 %collective-permute-start.17 = (f32[1,32,64]{2,1,0:T(8,128)}, f32[1,32,64]{2,1,0:T(8,128)S(1)}, u32[]{:S(2)}, u32[]{:S(2)}) collective-permute-start(f32[1,32,64]{2,1,0:T(8,128)} %broadcast.233), channel_id=1, source_target_pairs={{4,0},{8,4},{12,8},{16,12},{20,16},{24,20},{28,24},{32,28},{36,32}... | collective-permute-start | bytes 24584 | tf_op jit(solution)/shard_map/ppermute | solution.py:24
  9.0 35.6 %reshape.300 = f32[8,2,32,2,64,2]{5,4,3,2,1,0:T(8,128)} reshape(f32[16,64,128]{2,1,0:T(8,128)} %param.4) | data formatting | bytes 1048576 | tf_op jit(solution)/shard_map/reshape | solution.py:56
  44.6 12.2 %reduce_sum.87 = f32[8,32,64]{2,1,0:T(8,128)S(1)} reduce(f32[8,2,32,2,64,2]{5,4,3,2,1,0:T(8,128)} %reshape.300, f32[]{:T(128)} %constant.56.clone.1), dimensions={1,3,5}, to_apply=%region_1.0 | reduce | flops 114688 | bytes 589828 | tf_op jit(solution)/shard_map/reduce_sum | solution.py:56
  56.9 5.7 div.173
  62.6 2.6 reduce_sum.89
  67.0 5.1 collective-permute-start.64
  72.1 5.1 collective-permute-start.65
  91.2 5.0 collective-permute-start.48
  97.5 4.7 collective-permute-start.49
  103.2 4.7 collective-permute-start.32
  109.2 4.5 collective-permute-start.33
  115.6 5.1 collective-permute-start.16
  122.1 5.1 collective-permute-start
  128.0 5.1 collective-permute-start.1
  135.0 2.8 collective-permute-start.20
  160.7 2.5 copy.287
  165.9 8.4 %fusion.65 = (f32[16,64,128]{1,0,2:T(8,128)S(1)}, f32[16,64,128]{1,0,2:T(8,128)S(1)}, f32[16,64,128]{1,0,2:T(8,128)}, f32[16,64,128]{1,0,2:T(8,128)}, f32[16,64,...) fusion(f32[16,64,128]{1,0,2:T(8,128)} %copy-done.6, f32[16,64,128]{1,0,2:T(8,128)S(1)} %copy.238, ...), kind=kLoop, calls=%fused_computation.77 | loop fusion | flops 6422528 | bytes 11534336 | tf_op jit(solution)/shard_map/add | solution.py:51
  175.2 5.1 collective-permute-start.8
  184.1 3.3 collective-permute-start.10
  198.3 5.6 fusion.56
  204.5 5.1 collective-permute-start.12
  213.4 2.5 collective-permute-start.14
  221.9 2.5 copy.292
  224.4 2.4 copy.293
  226.8 5.7 fusion.43
  234.9 35.6 %reshape.299 = f32[8,2,32,2,64,2]{5,4,3,2,1,0:T(8,128)} reshape(f32[16,64,128]{2,1,0:T(8,128)} %copy.252) | data formatting | bytes 1048576 | tf_op jit(solution)/shard_map/reshape | solution.py:56
  270.5 12.2 %reduce_sum.86 = f32[8,32,64]{2,1,0:T(8,128)S(1)} reduce(f32[8,2,32,2,64,2]{5,4,3,2,1,0:T(8,128)} %reshape.299, f32[]{:T(128)} %constant.56.clone.1), dimensions={1,3,5}, to_apply=%region_0.0 | reduce | flops 114688 | bytes 589828 | tf_op jit(solution)/shard_map/reduce_sum | solution.py:56
  291.0 5.0 collective-permute-done.25
  296.1 3.2 collective-permute-start.26
  300.6 3.2 collective-permute-done.27
  305.6 5.1 collective-permute-done.29
  310.7 3.3 collective-permute-start.30
  318.5 6.6 reshape.301
  325.1 3.2 reduce_sum.88
  332.9 5.1 collective-permute-done.41
  338.1 2.6 collective-permute-start.42
  342.0 3.9 collective-permute-done.43
  348.2 5.1 collective-permute-done.45
  353.3 3.3 collective-permute-start.46
  369.4 5.1 collective-permute-done.57
  374.5 3.2 collective-permute-start.58
  382.8 5.1 collective-permute-done.61
  387.9 2.7 collective-permute-start.62
  400.1 5.1 collective-permute-done.73
  412.5 5.1 collective-permute-done.77
  417.6 2.9 collective-permute-start.78
  426.1 5.1 collective-permute-done.81
  438.2 5.5 collective-permute-done.85
  450.7 5.1 collective-permute-done.89
  462.8 5.1 collective-permute-done.93
  475.6 5.1 collective-permute-done.97
  492.9 5.2 collective-permute-done.101
  505.4 5.1 collective-permute-done.105
  523.5 5.1 collective-permute-done.109
  536.7 5.1 collective-permute-done.113
  556.0 5.3 collective-permute-done.117
  569.3 5.1 collective-permute-done.121
  585.3 5.1 collective-permute-start.124
  608.3 5.6 fusion.33
  614.3 5.1 collective-permute-start.128
  636.7 5.3 fusion.20
  642.2 5.1 collective-permute-start.132
  659.6 2.4 copy.298
  664.4 6.5 fusion.7
  (572 shorter events, 298.5 us)
Async XLA Ops:
  1.2 126.8 %collective-permute-start.17 = (f32[1,32,64]{2,1,0:T(8,128)}, f32[1,32,64]{2,1,0:T(8,128)S(1)}, u32[]{:S(2)}, u32[]{:S(2)}) collective-permute-start(f32[1,32,64]{2,1,0:T(8,128)} %broadcast.233), channel_id=1, source_target_pairs={{4,0},{8,4},{12,8},{16,12},{20,16},{24,20},{28,24},{32,28},{36,32}... | collective-permute-start | bytes 24584 | tf_op jit(solution)/shard_map/ppermute | solution.py:24
  9.0 124.2 %collective-permute-start.19 = (f32[1,32,64]{2,1,0:T(8,128)}, f32[1,32,64]{2,1,0:T(8,128)S(1)}, u32[]{:S(2)}, u32[]{:S(2)}) collective-permute-start(f32[1,32,64]{2,1,0:T(8,128)} %broadcast.233), channel_id=1, source_target_pairs={{0,4},{4,8},{8,12},{12,16},{16,20},{20,24},{24,28},{28,32},{32,36}... | collective-permute-start | bytes 24584 | tf_op jit(solution)/shard_map/ppermute | solution.py:21
  67.0 24.1 %collective-permute-start.64 = (f32[1,4,8]{2,1,0:T(4,128)S(1)}, f32[1,4,8]{2,1,0:T(4,128)S(1)}, u32[]{:S(2)}, u32[]{:S(2)}) collective-permute-start(f32[1,4,8]{2,1,0:T(4,128)S(1)} %multiply_bitcast_fusion), channel_id=1, source_target_pairs={{4,0},{8,4},{12,8},{16,12},{20,16},{24,20},{28,24},{32,28},{36,32}... | collective-permute-start | bytes 392 | tf_op jit(solution)/shard_map/ppermute | solution.py:24
  72.1 19.0 %collective-permute-start.66 = (f32[1,4,8]{2,1,0:T(4,128)S(1)}, f32[1,4,8]{2,1,0:T(4,128)S(1)}, u32[]{:S(2)}, u32[]{:S(2)}) collective-permute-start(f32[1,4,8]{2,1,0:T(4,128)S(1)} %multiply_bitcast_fusion), channel_id=1, source_target_pairs={{0,4},{4,8},{8,12},{12,16},{16,20},{20,24},{24,28},{28,32},{32,36}... | collective-permute-start | bytes 392 | tf_op jit(solution)/shard_map/ppermute | solution.py:21
  72.1 24.7 %collective-permute-start.65 = (f32[1,4,8]{2,1,0:T(4,128)S(1)}, f32[1,4,8]{2,1,0:T(4,128)S(1)}, u32[]{:S(2)}, u32[]{:S(2)}) collective-permute-start(f32[1,4,8]{2,1,0:T(4,128)S(1)} %broadcast_in_dim.66), channel_id=1, source_target_pairs={{4,0},{8,4},{12,8},{16,12},{20,16},{24,20},{28,24},{32,28},{36,32}... | collective-permute-start | bytes 392 | tf_op jit(solution)/shard_map/ppermute | solution.py:24
  91.1 6.4 collective-permute-start.67
  91.2 11.6 %collective-permute-start.48 = (f32[1,8,16]{2,1,0:T(8,128)S(1)}, f32[1,8,16]{2,1,0:T(8,128)S(1)}, u32[]{:S(2)}, u32[]{:S(2)}) collective-permute-start(f32[1,8,16]{2,1,0:T(8,128)S(1)} %get-tuple-element.244), channel_id=1, source_target_pairs={{4,0},{8,4},{12,8},{16,12},{20,16},{24,20},{28,24},{32,28},{36,32}... | collective-permute-start | bytes 1544 | tf_op jit(solution)/shard_map/ppermute | solution.py:24
  97.5 11.0 %collective-permute-start.49 = (f32[1,8,16]{2,1,0:T(8,128)S(1)}, f32[1,8,16]{2,1,0:T(8,128)S(1)}, u32[]{:S(2)}, u32[]{:S(2)}) collective-permute-start(f32[1,8,16]{2,1,0:T(8,128)S(1)} %broadcast.240), channel_id=1, source_target_pairs={{4,0},{8,4},{12,8},{16,12},{20,16},{24,20},{28,24},{32,28},{36,32}... | collective-permute-start | bytes 1544 | tf_op jit(solution)/shard_map/ppermute | solution.py:24
  103.2 11.2 %collective-permute-start.32 = (f32[1,16,32]{2,1,0:T(8,128)S(1)}, f32[1,16,32]{2,1,0:T(8,128)S(1)}, u32[]{:S(2)}, u32[]{:S(2)}) collective-permute-start(f32[1,16,32]{2,1,0:T(8,128)S(1)} %get-tuple-element.200), channel_id=1, source_target_pairs={{4,0},{8,4},{12,8},{16,12},{20,16},{24,20},{28,24},{32,28},{36,32}... | collective-permute-start | bytes 6152 | tf_op jit(solution)/shard_map/ppermute | solution.py:24
  108.5 6.5 collective-permute-start.34
  109.2 6.4 collective-permute-start.33
  114.3 6.4 collective-permute-start.35
  115.0 20.0 %collective-permute-start.2 = (f32[1,64,128]{2,1,0:T(8,128)}, f32[1,64,128]{2,1,0:T(8,128)S(1)}, u32[]{:S(2)}, u32[]{:S(2)}) collective-permute-start(f32[1,64,128]{2,1,0:T(8,128)} %get-tuple-element.115), channel_id=1, source_target_pairs={{0,4},{4,8},{8,12},{12,16},{16,20},{20,24},{24,28},{28,32},{32,36}... | collective-permute-start | bytes 98312 | tf_op jit(solution)/shard_map/ppermute | solution.py:21
  115.6 6.5 collective-permute-start.16
  120.8 6.6 collective-permute-start.18
  122.1 15.7 %collective-permute-start = (f32[1,64,128]{2,1,0:T(8,128)}, f32[1,64,128]{2,1,0:T(8,128)S(1)}, u32[]{:S(2)}, u32[]{:S(2)}) collective-permute-start(f32[1,64,128]{2,1,0:T(8,128)} %get-tuple-element.114), channel_id=1, source_target_pairs={{4,0},{8,4},{12,8},{16,12},{20,16},{24,20},{28,24},{32,28},{36,32}... | collective-permute-start | bytes 98312 | tf_op jit(solution)/shard_map/ppermute | solution.py:24
  127.3 11.6 %collective-permute-start.3 = (f32[1,64,128]{2,1,0:T(8,128)}, f32[1,64,128]{2,1,0:T(8,128)S(1)}, u32[]{:S(2)}, u32[]{:S(2)}) collective-permute-start(f32[1,64,128]{2,1,0:T(8,128)} %get-tuple-element.120), channel_id=1, source_target_pairs={{0,4},{4,8},{8,12},{12,16},{16,20},{20,24},{24,28},{28,32},{32,36}... | collective-permute-start | bytes 98312 | tf_op jit(solution)/shard_map/ppermute | solution.py:21
  128.0 13.0 %collective-permute-start.1 = (f32[1,64,128]{2,1,0:T(8,128)}, f32[1,64,128]{2,1,0:T(8,128)S(1)}, u32[]{:S(2)}, u32[]{:S(2)}) collective-permute-start(f32[1,64,128]{2,1,0:T(8,128)} %get-tuple-element.119), channel_id=1, source_target_pairs={{4,0},{8,4},{12,8},{16,12},{20,16},{24,20},{28,24},{32,28},{36,32}... | collective-permute-start | bytes 98312 | tf_op jit(solution)/shard_map/ppermute | solution.py:24
  133.2 264.6 %collective-permute-start.68 = (f32[3,1,8]{2,1,0:T(1,128)}, f32[3,1,8]{2,1,0:T(1,128)}, u32[]{:S(2)}, u32[]{:S(2)}) collective-permute-start(f32[3,1,8]{2,1,0:T(1,128)} %get-tuple-element.264), channel_id=1, source_target_pairs={{1,0},{2,1},{3,2},{0,3},{5,4},{6,5},{7,6},{4,7},{9,8},{10,9},{11,1... | collective-permute-start | bytes 296 | tf_op jit(solution)/shard_map/ppermute | solution.py:24
  135.0 147.8 %collective-permute-start.20 = (f32[10,1,64]{2,1,0:T(1,128)}, f32[10,1,64]{2,1,0:T(1,128)}, u32[]{:S(2)}, u32[]{:S(2)}) collective-permute-start(f32[10,1,64]{2,1,0:T(1,128)} %get-tuple-element.130), channel_id=1, source_target_pairs={{1,0},{2,1},{3,2},{0,3},{5,4},{6,5},{7,6},{4,7},{9,8},{10,9},{11,1... | collective-permute-start | bytes 7688 | tf_op jit(solution)/shard_map/ppermute | solution.py:24
  137.8 147.1 %collective-permute-start.22 = (f32[10,1,64]{2,1,0:T(1,128)}, f32[10,1,64]{2,1,0:T(1,128)}, u32[]{:S(2)}, u32[]{:S(2)}) collective-permute-start(f32[10,1,64]{2,1,0:T(1,128)} %get-tuple-element.129), channel_id=1, source_target_pairs={{0,1},{1,2},{2,3},{3,0},{4,5},{5,6},{6,7},{7,4},{8,9},{9,10},{10,1... | collective-permute-start | bytes 7688 | tf_op jit(solution)/shard_map/ppermute | solution.py:21
  138.9 12.7 %collective-permute-start.4 = (f32[18,1,128]{2,1,0:T(1,128)S(1)}, f32[18,1,128]{2,1,0:T(1,128)S(1)}, u32[]{:S(2)}, u32[]{:S(2)}) collective-permute-start(f32[18,1,128]{2,1,0:T(1,128)S(1)} %get-tuple-element.106), channel_id=1, source_target_pairs={{1,0},{2,1},{3,2},{0,3},{5,4},{6,5},{7,6},{4,7},{9,8},{10,9},{11,1... | collective-permute-start | bytes 27656 | tf_op jit(solution)/shard_map/ppermute | solution.py:24
  141.0 12.7 %collective-permute-start.6 = (f32[18,1,128]{2,1,0:T(1,128)S(1)}, f32[18,1,128]{2,1,0:T(1,128)S(1)}, u32[]{:S(2)}, u32[]{:S(2)}) collective-permute-start(f32[18,1,128]{2,1,0:T(1,128)S(1)} %get-tuple-element.105), channel_id=1, source_target_pairs={{0,1},{1,2},{2,3},{3,0},{4,5},{5,6},{6,7},{7,4},{8,9},{9,10},{10,1... | collective-permute-start | bytes 27656 | tf_op jit(solution)/shard_map/ppermute | solution.py:21
  175.2 7.8 %collective-permute-start.9 = (f32[1,64,128]{1,0,2:T(1,128)}, f32[1,64,128]{1,0,2:T(1,128)S(1)}, u32[]{:S(2)}, u32[]{:S(2)}) collective-permute-start(f32[1,64,128]{1,0,2:T(1,128)} %get-tuple-element.74), channel_id=1, source_target_pairs={{0,4},{4,8},{8,12},{12,16},{16,20},{20,24},{24,28},{28,32},{32,36}... | collective-permute-start | bytes 98312 | tf_op jit(solution)/shard_map/ppermute | solution.py:21
  175.2 7.9 %collective-permute-start.8 = (f32[1,64,128]{1,0,2:T(1,128)}, f32[1,64,128]{1,0,2:T(1,128)S(1)}, u32[]{:S(2)}, u32[]{:S(2)}) collective-permute-start(f32[1,64,128]{1,0,2:T(1,128)} %get-tuple-element.73), channel_id=1, source_target_pairs={{4,0},{8,4},{12,8},{16,12},{20,16},{24,20},{28,24},{32,28},{36,32}... | collective-permute-start | bytes 98312 | tf_op jit(solution)/shard_map/ppermute | solution.py:24
  204.0 8.3 %collective-permute-start.13 = (f32[1,64,128]{1,0,2:T(1,128)S(1)}, f32[1,64,128]{1,0,2:T(1,128)S(1)}, u32[]{:S(2)}, u32[]{:S(2)}) collective-permute-start(f32[1,64,128]{1,0,2:T(1,128)S(1)} %get-tuple-element.68), channel_id=1, source_target_pairs={{0,4},{4,8},{8,12},{12,16},{16,20},{20,24},{24,28},{28,32},{32,36}... | collective-permute-start | bytes 98312 | tf_op jit(solution)/shard_map/ppermute | solution.py:21
  204.5 7.9 %collective-permute-start.12 = (f32[1,64,128]{1,0,2:T(1,128)S(1)}, f32[1,64,128]{1,0,2:T(1,128)S(1)}, u32[]{:S(2)}, u32[]{:S(2)}) collective-permute-start(f32[1,64,128]{1,0,2:T(1,128)S(1)} %get-tuple-element.67), channel_id=1, source_target_pairs={{4,0},{8,4},{12,8},{16,12},{20,16},{24,20},{28,24},{32,28},{36,32}... | collective-permute-start | bytes 98312 | tf_op jit(solution)/shard_map/ppermute | solution.py:24
  217.3 67.6 %collective-permute-start.21 = (f32[10,1,64]{2,1,0:T(1,128)}, f32[10,1,64]{2,1,0:T(1,128)S(1)}, u32[]{:S(2)}, u32[]{:S(2)}) collective-permute-start(f32[10,1,64]{2,1,0:T(1,128)} %get-tuple-element.131), channel_id=1, source_target_pairs={{1,0},{2,1},{3,2},{0,3},{5,4},{6,5},{7,6},{4,7},{9,8},{10,9},{11,1... | collective-permute-start | bytes 7688 | tf_op jit(solution)/shard_map/ppermute | solution.py:24
  219.5 65.3 %collective-permute-start.23 = (f32[10,1,64]{2,1,0:T(1,128)}, f32[10,1,64]{2,1,0:T(1,128)S(1)}, u32[]{:S(2)}, u32[]{:S(2)}) collective-permute-start(f32[10,1,64]{2,1,0:T(1,128)} %get-tuple-element.132), channel_id=1, source_target_pairs={{0,1},{1,2},{2,3},{3,0},{4,5},{5,6},{6,7},{7,4},{8,9},{9,10},{10,1... | collective-permute-start | bytes 7688 | tf_op jit(solution)/shard_map/ppermute | solution.py:21
  282.8 45.5 %collective-permute-start.36 = (f32[6,1,32]{2,1,0:T(1,128)}, f32[6,1,32]{2,1,0:T(1,128)}, u32[]{:S(2)}, u32[]{:S(2)}) collective-permute-start(f32[6,1,32]{2,1,0:T(1,128)} %get-tuple-element.172), channel_id=1, source_target_pairs={{1,0},{2,1},{3,2},{0,3},{5,4},{6,5},{7,6},{4,7},{9,8},{10,9},{11,1... | collective-permute-start | bytes 2312 | tf_op jit(solution)/shard_map/ppermute | solution.py:24
  284.9 45.4 %collective-permute-start.38 = (f32[6,1,32]{2,1,0:T(1,128)}, f32[6,1,32]{2,1,0:T(1,128)}, u32[]{:S(2)}, u32[]{:S(2)}) collective-permute-start(f32[6,1,32]{2,1,0:T(1,128)} %get-tuple-element.171), channel_id=1, source_target_pairs={{0,1},{1,2},{2,3},{3,0},{4,5},{5,6},{6,7},{7,4},{8,9},{9,10},{10,1... | collective-permute-start | bytes 2312 | tf_op jit(solution)/shard_map/ppermute | solution.py:21
  289.6 6.5 collective-permute-start.25
  304.1 6.6 collective-permute-start.29
  315.4 14.9 %collective-permute-start.37 = (f32[6,1,32]{2,1,0:T(1,128)}, f32[6,1,32]{2,1,0:T(1,128)}, u32[]{:S(2)}, u32[]{:S(2)}) collective-permute-start(f32[6,1,32]{2,1,0:T(1,128)} %get-tuple-element.173), channel_id=1, source_target_pairs={{1,0},{2,1},{3,2},{0,3},{5,4},{6,5},{7,6},{4,7},{9,8},{10,9},{11,1... | collective-permute-start | bytes 2312 | tf_op jit(solution)/shard_map/ppermute | solution.py:24
  317.6 12.6 %collective-permute-start.39 = (f32[6,1,32]{2,1,0:T(1,128)}, f32[6,1,32]{2,1,0:T(1,128)}, u32[]{:S(2)}, u32[]{:S(2)}) collective-permute-start(f32[6,1,32]{2,1,0:T(1,128)} %get-tuple-element.174), channel_id=1, source_target_pairs={{0,1},{1,2},{2,3},{3,0},{4,5},{5,6},{6,7},{7,4},{8,9},{9,10},{10,1... | collective-permute-start | bytes 2312 | tf_op jit(solution)/shard_map/ppermute | solution.py:21
  328.3 36.5 %collective-permute-start.52 = (f32[4,1,16]{2,1,0:T(1,128)}, f32[4,1,16]{2,1,0:T(1,128)}, u32[]{:S(2)}, u32[]{:S(2)}) collective-permute-start(f32[4,1,16]{2,1,0:T(1,128)} %get-tuple-element.214), channel_id=1, source_target_pairs={{1,0},{2,1},{3,2},{0,3},{5,4},{6,5},{7,6},{4,7},{9,8},{10,9},{11,1... | collective-permute-start | bytes 776 | tf_op jit(solution)/shard_map/ppermute | solution.py:24
  330.3 35.2 %collective-permute-start.54 = (f32[4,1,16]{2,1,0:T(1,128)}, f32[4,1,16]{2,1,0:T(1,128)}, u32[]{:S(2)}, u32[]{:S(2)}) collective-permute-start(f32[4,1,16]{2,1,0:T(1,128)} %get-tuple-element.213), channel_id=1, source_target_pairs={{0,1},{1,2},{2,3},{3,0},{4,5},{5,6},{6,7},{7,4},{8,9},{9,10},{10,1... | collective-permute-start | bytes 776 | tf_op jit(solution)/shard_map/ppermute | solution.py:21
  331.6 6.5 collective-permute-start.41
  346.8 6.5 collective-permute-start.45
  357.9 9.0 %collective-permute-start.53 = (f32[4,1,16]{2,1,0:T(1,128)}, f32[4,1,16]{2,1,0:T(1,128)}, u32[]{:S(2)}, u32[]{:S(2)}) collective-permute-start(f32[4,1,16]{2,1,0:T(1,128)} %get-tuple-element.215), channel_id=1, source_target_pairs={{1,0},{2,1},{3,2},{0,3},{5,4},{6,5},{7,6},{4,7},{9,8},{10,9},{11,1... | collective-permute-start | bytes 776 | tf_op jit(solution)/shard_map/ppermute | solution.py:24
  360.2 6.7 %collective-permute-start.55 = (f32[4,1,16]{2,1,0:T(1,128)}, f32[4,1,16]{2,1,0:T(1,128)}, u32[]{:S(2)}, u32[]{:S(2)}) collective-permute-start(f32[4,1,16]{2,1,0:T(1,128)} %get-tuple-element.216), channel_id=1, source_target_pairs={{0,1},{1,2},{2,3},{3,0},{4,5},{5,6},{6,7},{7,4},{8,9},{9,10},{10,1... | collective-permute-start | bytes 776 | tf_op jit(solution)/shard_map/ppermute | solution.py:21
  364.8 33.0 %collective-permute-start.70 = (f32[3,1,8]{2,1,0:T(1,128)}, f32[3,1,8]{2,1,0:T(1,128)}, u32[]{:S(2)}, u32[]{:S(2)}) collective-permute-start(f32[3,1,8]{2,1,0:T(1,128)} %get-tuple-element.263), channel_id=1, source_target_pairs={{0,1},{1,2},{2,3},{3,0},{4,5},{5,6},{6,7},{7,4},{8,9},{9,10},{10,1... | collective-permute-start | bytes 296 | tf_op jit(solution)/shard_map/ppermute | solution.py:21
  365.4 32.3 %collective-permute-start.69 = (f32[3,1,8]{2,1,0:T(1,128)}, f32[3,1,8]{2,1,0:T(1,128)}, u32[]{:S(2)}, u32[]{:S(2)}) collective-permute-start(f32[3,1,8]{2,1,0:T(1,128)} %get-tuple-element.265), channel_id=1, source_target_pairs={{1,0},{2,1},{3,2},{0,3},{5,4},{6,5},{7,6},{4,7},{9,8},{10,9},{11,1... | collective-permute-start | bytes 296 | tf_op jit(solution)/shard_map/ppermute | solution.py:24
  368.1 6.4 collective-permute-start.57
  381.5 6.4 collective-permute-start.61
  398.8 6.4 collective-permute-start.73
  411.2 6.4 collective-permute-start.77
  424.8 6.4 collective-permute-start.81
  436.9 6.8 %collective-permute-start.85 = (f32[1,4,8]{2,1,0:T(4,128)S(1)}, f32[1,4,8]{2,1,0:T(4,128)S(1)}, u32[]{:S(2)}, u32[]{:S(2)}) collective-permute-start(f32[1,4,8]{2,1,0:T(4,128)S(1)} %divide_add_fusion.3), channel_id=1, source_target_pairs={{0,4},{4,8},{8,12},{12,16},{16,20},{20,24},{24,28},{28,32},{32,36}... | collective-permute-start | bytes 392 | tf_op jit(solution)/shard_map/ppermute | solution.py:21
  449.4 6.4 collective-permute-start.89
  461.5 6.4 collective-permute-start.93
  474.3 6.4 collective-permute-start.97
  491.6 6.5 collective-permute-start.101
  504.0 6.4 collective-permute-start.105
  522.2 6.5 collective-permute-start.109
  535.4 6.5 collective-permute-start.113
  554.6 6.8 %collective-permute-start.117 = (f32[1,32,64]{2,1,0:T(8,128)S(1)}, f32[1,32,64]{2,1,0:T(8,128)S(1)}, u32[]{:S(2)}, u32[]{:S(2)}) collective-permute-start(f32[1,32,64]{2,1,0:T(8,128)S(1)} %get-tuple-element.143), channel_id=1, source_target_pairs={{0,4},{4,8},{8,12},{12,16},{16,20},{20,24},{24,28},{28,32},{32,36}... | collective-permute-start | bytes 24584 | tf_op jit(solution)/shard_map/ppermute | solution.py:21
  567.8 6.6 collective-permute-start.121
  585.2 9.1 %collective-permute-start.125 = (f32[1,64,128]{1,0,2:T(1,128)S(1)}, f32[1,64,128]{1,0,2:T(1,128)S(1)}, u32[]{:S(2)}, u32[]{:S(2)}) collective-permute-start(f32[1,64,128]{1,0,2:T(1,128)S(1)} %get-tuple-element.62), channel_id=1, source_target_pairs={{0,4},{4,8},{8,12},{12,16},{16,20},{20,24},{24,28},{28,32},{32,36}... | collective-permute-start | bytes 98312 | tf_op jit(solution)/shard_map/ppermute | solution.py:21
  585.3 9.1 %collective-permute-start.124 = (f32[1,64,128]{1,0,2:T(1,128)S(1)}, f32[1,64,128]{1,0,2:T(1,128)S(1)}, u32[]{:S(2)}, u32[]{:S(2)}) collective-permute-start(f32[1,64,128]{1,0,2:T(1,128)S(1)} %get-tuple-element.61), channel_id=1, source_target_pairs={{4,0},{8,4},{12,8},{16,12},{20,16},{24,20},{28,24},{32,28},{36,32}... | collective-permute-start | bytes 98312 | tf_op jit(solution)/shard_map/ppermute | solution.py:24
  614.0 9.4 %collective-permute-start.129 = (f32[1,64,128]{1,0,2:T(1,128)S(1)}, f32[1,64,128]{1,0,2:T(1,128)S(1)}, u32[]{:S(2)}, u32[]{:S(2)}) collective-permute-start(f32[1,64,128]{1,0,2:T(1,128)S(1)} %get-tuple-element.56), channel_id=1, source_target_pairs={{0,4},{4,8},{8,12},{12,16},{16,20},{20,24},{24,28},{28,32},{32,36}... | collective-permute-start | bytes 98312 | tf_op jit(solution)/shard_map/ppermute | solution.py:21
  614.3 9.1 %collective-permute-start.128 = (f32[1,64,128]{1,0,2:T(1,128)S(1)}, f32[1,64,128]{1,0,2:T(1,128)S(1)}, u32[]{:S(2)}, u32[]{:S(2)}) collective-permute-start(f32[1,64,128]{1,0,2:T(1,128)S(1)} %get-tuple-element.55), channel_id=1, source_target_pairs={{4,0},{8,4},{12,8},{16,12},{20,16},{24,20},{28,24},{32,28},{36,32}... | collective-permute-start | bytes 98312 | tf_op jit(solution)/shard_map/ppermute | solution.py:24
  642.1 9.1 %collective-permute-start.133 = (f32[1,64,128]{1,0,2:T(1,128)S(1)}, f32[1,64,128]{1,0,2:T(1,128)S(1)}, u32[]{:S(2)}, u32[]{:S(2)}) collective-permute-start(f32[1,64,128]{1,0,2:T(1,128)S(1)} %get-tuple-element.50), channel_id=1, source_target_pairs={{0,4},{4,8},{8,12},{12,16},{16,20},{20,24},{24,28},{28,32},{32,36}... | collective-permute-start | bytes 98312 | tf_op jit(solution)/shard_map/ppermute | solution.py:21
  642.2 9.1 %collective-permute-start.132 = (f32[1,64,128]{1,0,2:T(1,128)S(1)}, f32[1,64,128]{1,0,2:T(1,128)S(1)}, u32[]{:S(2)}, u32[]{:S(2)}) collective-permute-start(f32[1,64,128]{1,0,2:T(1,128)S(1)} %get-tuple-element.49), channel_id=1, source_target_pairs={{4,0},{8,4},{12,8},{16,12},{20,16},{24,20},{28,24},{32,28},{36,32}... | collective-permute-start | bytes 98312 | tf_op jit(solution)/shard_map/ppermute | solution.py:24
  (128 other events, 1638.5 us)
where the time goes:
time: 686 us; the launch traced here: 674 us
  local copies, waits for them, and re-layouts  190 us (28%)
  waiting for transfers between devices  187 us (27%)
  starting transfers between devices  171 us (25%)
  other arithmetic  123 us (18%)
    ppermute x68, starting transfers between devices, with_halo(): lax.ppermute(lax.slice_in_dim(block, 0, width, axis=dim), axis, backward)  150 us
    ppermute x68, waiting for transfers between devices, with_halo(): lax.ppermute(lax.slice_in_dim(block, block.shape[dim] - width, None, axis...  140 us
    reshape x4, local copies, waits for them, and re-layouts, coarsen(): field.reshape(sx // 2, 2, sy // 2, 2, sz // 2, 2).mean(axis=(1, 3, 5))  79.7 us
    unnamed x137, local copies, waits for them, and re-layouts  50.4 us
    ppermute x68, waiting for transfers between devices, with_halo(): lax.ppermute(lax.slice_in_dim(block, 0, width, axis=dim), axis, backward)  46.7 us
    add x20, other arithmetic, relax(): return padded_press[1:-1, 1:-1] + OMEGA * (source_part - applied) / diagonal  37.8 us
    reduce_sum x10, other arithmetic, coarsen(): field.reshape(sx // 2, 2, sy // 2, 2, sz // 2, 2).mean(axis=(1, 3, 5))  33.6 us
    ppermute x68, starting transfers between devices, with_halo(): lax.ppermute(lax.slice_in_dim(block, block.shape[dim] - width, None, axis...  20.9 us
  transfers between devices with their start and end apart: 136, of which 91 were waited for; matrix products, arithmetic and copies ran while one was open for 34% of the time, Pallas kernels for 0%

commit v1 on v0

v1 whole, which is shorter than its diff:
```python
import functools

import jax
import jax.numpy as jnp
from jax import lax
from jax.experimental import pallas as pl
from jax.experimental.pallas import tpu as pltpu
from jax.sharding import PartitionSpec as P

MESH = pl.DeviceIdType.MESH
F32 = jnp.float32
OMEGA = 0.8
LANES = 128
SIDES = ((-1, 0), (1, 0), (0, -1), (0, 1), (-1, -1), (-1, 1), (1, -1), (1, 1))
REACH_G = 10
REACH_K = 11
SLOTS = 24
PEERS_K = [o for d in range(REACH_K, 0, -1) for o in (d, -d)]
PEERS_G = [o for d in range(REACH_G, 0, -1) for o in (d, -d)]


def recip(x):
    y = pl.reciprocal(x, approx=True)
    return y * (2.0 - x * y)


def roll(x, shift, axis):
    return pltpu.roll(x, shift % x.shape[axis], axis)


def loop(lo, hi, body):
    def step(i, carry):
        body(i)
        return carry

    lax.fori_loop(lo, hi, step, 0)


def strips(lo, hi, size=16):
    return [(r, min(size, hi - r)) for r in range(lo, hi, size)]


def lane_index(shape):
    return lax.broadcasted_iota(jnp.int32, shape, 1)


def pair_sum_z(x, s):
    first = (lane_index(x.shape) // s) % 2 == 0
    return x + jnp.where(first, roll(x, -s, 1), roll(x, s, 1))


class Level:
    def __init__(self, s, scale, k, r, fx, fy, fz, w, d):
        self.s, self.scale, self.k = s, scale, k
        self.r, self.fx, self.fy, self.fz, self.w, self.d = r, fx, fy, fz, w, d

    def inverses(self, planes, rows):
        def body(x):
            for r, n in rows:
                self.r[x, pl.ds(r, n), :] = (0.5 / self.scale) * recip(self.k[x, pl.ds(r, n), :])

        loop(*planes, body)

    def faces(self, planes, rows):
        def body(x):
            for r, n in rows:
                here = self.r[x, pl.ds(r, n), :]
                self.fx[x, pl.ds(r, n), :] = recip(here + self.r[x + 1, pl.ds(r, n), :])
                self.fy[x, pl.ds(r, n), :] = recip(here + self.r[x, pl.ds(r + 1, n), :])
                self.fz[x, pl.ds(r, n), :] = recip(here + roll(here, -self.s, 1))

        loop(*planes, body)

    def diagonal(self, planes, rows):
        def body(x):
            for r, n in rows:
                fz = self.fz[x, pl.ds(r, n), :]
                d = self.fx[x, pl.ds(r, n), :] + self.fx[x - 1, pl.ds(r, n), :]
                d += self.fy[x, pl.ds(r, n), :] + self.fy[x, pl.ds(r - 1, n), :]
                d += fz + roll(fz, self.s, 1)
                self.d[x, pl.ds(r, n), :] = d
                self.w[x, pl.ds(r, n), :] = OMEGA * recip(d)

        loop(*planes, body)

    def around(self, v, x, r, n):
        here = v[x, pl.ds(r, n), :]
        fz = self.fz[x, pl.ds(r, n), :]
        a = self.fx[x, pl.ds(r, n), :] * v[x + 1, pl.ds(r, n), :]
        a += self.fx[x - 1, pl.ds(r, n), :] * v[x - 1, pl.ds(r, n), :]
        a += self.fy[x, pl.ds(r, n), :] * v[x, pl.ds(r + 1, n), :]
        a += self.fy[x, pl.ds(r - 1, n), :] * v[x, pl.ds(r - 1, n), :]
        a += fz * roll(here, -self.s, 1) + roll(fz * here, self.s, 1)
        return here, a

    def first_sweep(self, g, dst, planes, rows):
        def body(x):
            for r, n in rows:
                dst[x, pl.ds(r, n), :] = self.w[x, pl.ds(r, n), :] * g[x, pl.ds(r, n), :]

        loop(*planes, body)

    def sweep(self, src, g, dst, planes, rows):
        def body(x):
            for r, n in rows:
                here, a = self.around(src, x, r, n)
                w = self.w[x, pl.ds(r, n), :]
                dst[x, pl.ds(r, n), :] = (1.0 - OMEGA) * here + w * (g[x, pl.ds(r, n), :] + a)

        loop(*planes, body)

    def residual(self, v, g, x, r, n):
        here, a = self.around(v, x, r, n)
        return g[x, pl.ds(r, n), :] + a - self.d[x, pl.ds(r, n), :] * here


def coarsen(value, s, tmp, dst, pairs, rows, dst_rows):
    lo, hi, plane = pairs

    def gather(j):
        x = plane(j)
        for r, n in rows:
            tmp[j, pl.ds(r, n), :] = pair_sum_z(value(x, r, n) + value(x + 1, r, n), s)

    loop(lo, hi, gather)
    first, count = rows[0][0], sum(n for _, n in rows) // 2

    def squeeze(j):
        even = tmp[j, pl.ds(first, count, stride=2), :]
        odd = tmp[j, pl.ds(first + 1, count, stride=2), :]
        dst[j, pl.ds(dst_rows, count), :] = 0.125 * (even + odd)

    loop(lo, hi, squeeze)


class Packed3:
    def __init__(self, shape):
        lane = lane_index(shape)
        self.y_last, self.y_first = lane >= 112, lane < 16
        self.z_last, self.z_first = lane % 16 == 15, lane % 16 == 0

    def y_next(self, v):
        t = [roll(a, -16, 1) for a in v]
        return [jnp.where(self.y_last, t[(i + 2) % 8], t[i]) for i in range(8)]

    def y_prev(self, v):
        t = [roll(a, 16, 1) for a in v]
        return [jnp.where(self.y_first, t[(i - 2) % 8], t[i]) for i in range(8)]

    def z_next(self, v):
        return [jnp.where(self.z_last, roll(a, 15, 1), roll(a, -1, 1)) for a in v]

    def z_prev(self, v):
        return [jnp.where(self.z_first, roll(a, -15, 1), roll(a, 1, 1)) for a in v]

    def x_next(self, v):
        return [v[i + 1] if i % 2 == 0 else roll(v[i - 1], -1, 0) for i in range(8)]

    def x_prev(self, v):
        return [roll(v[i + 1], 1, 0) if i % 2 == 0 else v[i - 1] for i in range(8)]

    def both(self, f, v):
        out = None
        for axis in range(3):
            nxt = (self.x_next, self.y_next, self.z_next)[axis](v)
            prv = (self.x_prev, self.y_prev, self.z_prev)[axis]([a * b for a, b in zip(f[axis], v)])
            term = [a * b + c for a, b, c in zip(f[axis], nxt, prv)]
            out = term if out is None else [a + b for a, b in zip(out, term)]
        return out


class Packed4(Packed3):
    def __init__(self, shape):
        lane = lane_index(shape)
        self.z_last, self.z_first = lane % 8 == 7, lane % 8 == 0

    def y_next(self, v):
        return [roll(v[0], -8, 1)]

    def y_prev(self, v):
        return [roll(v[0], 8, 1)]

    def z_next(self, v):
        return [jnp.where(self.z_last, roll(v[0], 7, 1), roll(v[0], -1, 1))]

    def z_prev(self, v):
        return [jnp.where(self.z_first, roll(v[0], -7, 1), roll(v[0], 1, 1))]

    def x_next(self, v):
        return [roll(v[0], -1, 0)]

    def x_prev(self, v):
        return [roll(v[0], 1, 0)]


def packed_coefs(pack, k, scale):
    r = [(0.5 / scale) * recip(a) for a in k]
    f = []
    d = None
    for nxt, prv in ((pack.x_next, pack.x_prev), (pack.y_next, pack.y_prev), (pack.z_next, pack.z_prev)):
        face = [recip(a + b) for a, b in zip(r, nxt(r))]
        f.append(face)
        both = [a + b for a, b in zip(face, prv(face))]
        d = both if d is None else [a + b for a, b in zip(d, both)]
    return f, d


def packed_sweep(pack, f, w, v, g):
    return [
        (1.0 - OMEGA) * a + b * (c + e) for a, b, c, e in zip(v, w, g, pack.both(f, v))
    ]


def dot(a, b):
    return jnp.dot(a, b, precision=lax.Precision.HIGHEST, preferred_element_type=F32)


def grid2(shape):
    return lax.broadcasted_iota(jnp.int32, shape, 0), lax.broadcasted_iota(jnp.int32, shape, 1)


def pack_rows(cells):
    l, t = grid2((LANES, LANES))
    choose = jnp.where((l // 8 == t % 16) & (l % 4 == 0), 0.125, 0.0).astype(F32)
    r, t = grid2((16, LANES))
    keep = r // 2 == t // 16
    rows = []
    for p in range(2):
        u = dot(cells[2 * p] + cells[2 * p + 1], choose)
        rows.append(jnp.sum(jnp.where(keep, u, 0.0), axis=0, keepdims=True))
    return rows


def kernel(
    ngx, ngy, p_hbm, k_hbm, s_hbm, v_out, r_out,
    w0, r0, fx0, fy0, fz0, wt0, d0, va0, vb0, vs0, res0,
    k1, r1, fx1, fy1, fz1, wt1, d1, g1, va1, vb1, dup1,
    k2, r2, fx2, fy2, fz2, wt2, d2, g2, va2, vb2, w2, dup2,
    tmp1, tmp2, yk, yg, xk, xg, c3, c4, v3,
    load_sem, store_sem, side_s, side_r, y_s, y_r, xk_s, xk_r, xg_s, xg_r,
):
    gx, gy = lax.axis_index("gx"), lax.axis_index("gy")

    def peer(dx, dy):
        return (lax.rem(gx + (dx + ngx), ngx), lax.rem(gy + (dy + ngy), ngy))

    loads = [
        pltpu.make_async_copy(hbm, w0.at[i, pl.ds(3, 16), pl.ds(16, 64), :], load_sem.at[i])
        for i, hbm in ((1, k_hbm), (0, p_hbm), (2, s_hbm))
    ]
    for c in loads:
        c.start()

    greet = list(SIDES) + [(0, 2)] + [(o, 0) for o in PEERS_K if abs(o) > 1]
    barrier = pltpu.get_barrier_semaphore()
    for o in greet:
        pl.semaphore_signal(barrier, inc=1, device_id=peer(*o), device_id_type=MESH)

    waits = []

    def exchange(which, src, dst, x0, nx, hx, ny):
        y0, hy = 16, 8
        lead = (slice(None),) * (len(src.shape) - 3)
        copies = []
        for i, (dx, dy) in enumerate(SIDES):
            xs, xd, xn = ((x0, x0 + nx, hx), (x0, x0, nx), (x0 + nx - hx, x0 - hx, hx))[dx + 1]
            ys, yd, yn = ((y0, y0 + ny, hy), (y0, y0, ny), (y0 + ny - hy, y0 - hy, hy))[dy + 1]
            c = pltpu.make_async_remote_copy(
                src_ref=src.at[lead + (pl.ds(xs, xn), pl.ds(ys, yn))],
                dst_ref=dst.at[lead + (pl.ds(xd, xn), pl.ds(yd, yn))],
                send_sem=side_s.at[which, i], recv_sem=side_r.at[which, i],
                device_id=peer(dx, dy), device_id_type=MESH,
            )
            c.start()
            copies.append(c)
        waits.extend(copies)
        return copies

    def gather_y(which, buf):
        copies = []
        for o in (1, 2, 3):
            c = pltpu.make_async_remote_copy(
                src_ref=buf.at[gy], dst_ref=buf.at[gy],
                send_sem=y_s.at[which, o - 1], recv_sem=y_r.at[which, o - 1],
                device_id=peer(0, o), device_id_type=MESH,
            )
            c.start()
            copies.append(c)
        waits.extend(copies)
        return copies

    def gather_x(buf, peers, send, recv):
        copies = []
        for i, o in enumerate(peers):
            c = pltpu.make_async_remote_copy(
                src_ref=buf.at[pl.ds(8 * REACH_K, 8), :], dst_ref=buf.at[pl.ds(8 * (REACH_K - o), 8), :],
                send_sem=send.at[i], recv_sem=recv.at[i],
                device_id=peer(o, 0), device_id_type=MESH,
            )
            c.start()
            copies.append(c)
        waits.extend(copies)
        return copies

    def arrive(copies):
        for c in copies:
            c.wait_recv()

    press, coef, source = w0.at[0], w0.at[1], w0.at[2]
    l0 = Level(1, 1.0, coef, r0, fx0, fy0, fz0, wt0, d0)
    l1 = Level(2, 0.25, k1, r1, fx1, fy1, fz1, wt1, d1)
    l2 = Level(4, 0.0625, k2, r2, fx2, fy2, fz2, wt2, d2)
    all0, own0 = strips(8, 88), strips(16, 80)
    all1, own1 = strips(8, 56), strips(16, 48)
    all2 = strips(8, 40)

    loads[0].wait()
    coarsen(lambda x, r, n: coef[x, pl.ds(r, n), :], 1, tmp1, k1, (8, 16, lambda j: 2 * j - 13), own0, 16)
    coarsen(lambda x, r, n: k1[x, pl.ds(r, n), :], 2, tmp2, k2, (4, 8, lambda j: 2 * j), own1, 16)
    for p, row in enumerate(pack_rows([k2[4 + i, pl.ds(16, 16), :] for i in range(4)])):
        yk[gy, pl.ds(p, 1), :] = row
    loads[1].wait()
    loads[2].wait()

    pl.semaphore_wait(barrier, len(greet))
    a_in = exchange(0, w0, w0, 3, 16, 3, 64)
    k1_in = exchange(1, k1, k1, 8, 8, 8, 32)
    yk_in = gather_y(0, yk)

    arrive(yk_in)
    for i in range(4):
        xk[pl.ds(8 * REACH_K + 2 * i, 2), :] = yk[i, pl.ds(0, 2), :]
    xk_in = gather_x(xk, PEERS_K, xk_s, xk_r)

    arrive(a_in)
    l0.inverses((0, 22), all0)
    l0.faces((0, 21), all0)
    l0.diagonal((1, 21), all0)
    l0.sweep(press, source, va0, (1, 21), all0)
    l0.sweep(va0, source, vb0, (2, 20), all0)
    coarsen(
        functools.partial(l0.residual, vb0, source), 1, tmp1, g1, (8, 16, lambda j: 2 * j - 13), own0, 16
    )
    g1_in = exchange(2, g1, g1, 8, 8, 6, 32)
    v0_in = exchange(3, vb0, vs0, 3, 16, 3, 64)

    arrive(k1_in)
    l1.inverses((0, 24), all1)
    l1.faces((0, 23), all1)
    l1.diagonal((1, 23), all1)
    coarsen(lambda x, r, n: k1[x, pl.ds(r, n), :], 2, tmp2, k2, (0, 12, lambda j: 2 * j), strips(0, 64), 8)
    l2.inverses((0, 12), all2)
    l2.faces((0, 11), all2)
    l2.diagonal((1, 11), all2)

    def keep(x):
        for r, n in own0:
            vs0[x, pl.ds(r, n), :] = vb0[x, pl.ds(r, n), :]

    loop(3, 19, keep)

    arrive(xk_in)
    shape = (SLOTS, LANES)
    pack3, pack4 = Packed3(shape), Packed4(shape)
    kk = [xk[pl.ds(i, SLOTS, stride=8), :] for i in range(8)]
    f, d = packed_coefs(pack3, kk, 1.0 / 64)
    for i in range(8):
        for j, value in enumerate((f[0][i], f[1][i], f[2][i], OMEGA * recip(d[i]), d[i])):
            c3[j, i] = value
    l, t = grid2((LANES, LANES))

    def squeeze(values):
        out = None
        for i in range(4):
            y = t // 8 - 4 * i
            choose = jnp.where((l // 32 == y) & ((l % 16) // 2 == t % 8), 0.125, 0.0).astype(F32)
            part = dot(values[2 * i] + values[2 * i + 1], choose)
            out = part if out is None else out + part
        return out

    f, d = packed_coefs(pack4, [squeeze(kk)], 1.0 / 256)
    for j, value in enumerate((f[0][0], f[1][0], f[2][0], OMEGA * recip(d[0]))):
        c4[j] = value

    arrive(g1_in)
    l1.first_sweep(g1, va1, (2, 22), all1)
    l1.sweep(va1, g1, vb1, (3, 21), all1)
    coarsen(
        functools.partial(l1.residual, vb1, g1), 2, tmp2, g2, (2, 10, lambda j: 2 * j), all1, 12
    )
    l2.first_sweep(g2, va2, (2, 10), all2)
    l2.sweep(va2, g2, vb2, (3, 9), all2)
    cells = [l2.residual(vb2, g2, 4 + i, 16, 16) for i in range(4)]
    for p, row in enumerate(pack_rows(cells)):
        yg[gy, pl.ds(p, 1), :] = row
    yg_in = gather_y(1, yg)
    for x in range(4, 8):
        w2[0, x, pl.ds(16, 16), :] = vb2[x, pl.ds(16, 16), :]
        w2[1, x, pl.ds(16, 16), :] = g2[x, pl.ds(16, 16), :]
    w2_in = exchange(4, w2, w2, 4, 4, 4, 16)
    arrive(yg_in)
    for i in range(4):
        xg[pl.ds(8 * REACH_K + 2 * i, 2), :] = yg[i, pl.ds(0, 2), :]
    xg_in = gather_x(xg, PEERS_G, xg_s, xg_r)
    arrive(xg_in)

    g3 = [xg[pl.ds(i, SLOTS, stride=8), :] for i in range(8)]
    f3 = [[c3[j, i] for i in range(8)] for j in range(3)]
    wt3 = [c3[3, i] for i in range(8)]
    saved = [a * b for a, b in zip(wt3, g3)]
    saved = packed_sweep(pack3, f3, wt3, saved, g3)
    around = pack3.both(f3, saved)
    g4 = squeeze([g3[i] + around[i] - c3[4, i] * saved[i] for i in range(8)])
    f4, wt4 = [[c4[j]] for j in range(3)], [c4[3]]

    def coarsest(_, v):
        return packed_sweep(pack4, f4, wt4, [v], [g4])[0]

    v4 = lax.fori_loop(0, 7, coarsest, wt4[0] * g4)
    v = []
    for i in range(4):
        y = l // 8 - 4 * i
        spread = jnp.where((t // 32 == y) & ((t % 16) // 2 == l % 8), 1.0, 0.0).astype(F32)
        part = dot(v4, spread)
        v += [saved[2 * i] + part, saved[2 * i + 1] + part]
    for _ in range(2):
        v = packed_sweep(pack3, f3, wt3, v, g3)
    for i in range(8):
        v3[i] = v[i]

    r, t8 = grid2((8, LANES))
    low = lax.rem(gy + (ngy - 1), ngy)
    high = lax.rem(gy + 1, ngy)
    parts = []
    for j in range(6):
        slot, p = REACH_K - 1 + j // 2, j % 2
        for part, y in ((low, 4), (gy, 0), (gy, 4), (high, 0)):
            row = jnp.broadcast_to(v3[2 * part + p, pl.ds(slot, 1), :], (8, LANES))
            parts.append(jnp.where(t8 // 16 == r // 2 + y, row, 0.0))
    spread = jnp.where(l % 16 == t // 8, 1.0, 0.0).astype(F32)
    fine = dot(jnp.concatenate(parts, axis=0), spread)
    for j in range(6):
        dup2[j] = fine[32 * j : 32 * j + 32]

    arrive(w2_in)

    def correct2(x):
        va2[x, pl.ds(8, 32), :] = w2[0, x, pl.ds(8, 32), :] + dup2[x // 2]

    loop(0, 12, correct2)
    l2.sweep(va2, w2.at[1], vb2, (1, 11), all2)
    l2.sweep(vb2, w2.at[1], va2, (2, 10), all2)

    def double2(x):
        c = va2[x, pl.ds(12, 24), :]
        dup1[x, pl.ds(8, 24, stride=2), :] = c
        dup1[x, pl.ds(9, 24, stride=2), :] = c

    loop(2, 10, double2)

    def correct1(x):
        for r, n in all1:
            va1[x, pl.ds(r, n), :] = vb1[x, pl.ds(r, n), :] + dup1[x // 2, pl.ds(r, n), :]

    loop(4, 20, correct1)
    l1.sweep(va1, g1, vb1, (5, 19), all1)
    l1.sweep(vb1, g1, va1, (6, 18), all1)

    def double1(x):
        c = va1[x, pl.ds(12, 40), :]
        tmp1[x, pl.ds(8, 40, stride=2), :] = c
        tmp1[x, pl.ds(9, 40, stride=2), :] = c

    loop(6, 18, double1)
    arrive(v0_in)
    for c in v0_in:
        c.wait_send()

    def correct0(x):
        for r, n in all0:
            va0[x, pl.ds(r, n), :] = vs0[x, pl.ds(r, n), :] + tmp1[(x + 13) // 2, pl.ds(r, n), :]

    loop(0, 22, correct0)
    l0.sweep(va0, source, vb0, (1, 21), all0)
    l0.sweep(vb0, source, va0, (2, 20), all0)
    v_store = pltpu.make_async_copy(va0.at[pl.ds(3, 16), pl.ds(16, 64), :], v_out, store_sem.at[0])
    v_store.start()

    def final(x):
        for r, n in own0:
            res0[x - 3, pl.ds(r - 16, n), :] = l0.residual(va0, source, x, r, n)

    loop(3, 19, final)
    r_store = pltpu.make_async_copy(res0, r_out, store_sem.at[1])
    r_store.start()
    done = [id(c) for c in v0_in]
    for c in waits:
        if id(c) not in done:
            c.wait_send()
    v_store.wait()
    r_store.wait()


def solution(mesh):
    ngx, ngy = mesh.shape["gx"], mesh.shape["gy"]

    def vmem(*shape):
        return pltpu.VMEM(shape, F32)

    n0, n1, n2 = (22, 96, LANES), (24, 64, LANES), (12, 48, LANES)
    scratch = [vmem(3, *n0)] + [vmem(*n0)] * 9 + [vmem(16, 64, LANES)]
    scratch += [vmem(*n1)] * 10 + [vmem(12, 64, LANES)]
    scratch += [vmem(*n2)] * 10 + [vmem(2, *n2), vmem(6, 32, LANES)]
    scratch += [vmem(18, 96, LANES), vmem(12, 64, LANES)]
    scratch += [vmem(4, 8, LANES)] * 2 + [vmem(8 * SLOTS, LANES)] * 2
    scratch += [vmem(5, 8, SLOTS, LANES), vmem(4, SLOTS, LANES), vmem(8, SLOTS, LANES)]
    dma = pltpu.SemaphoreType.DMA
    scratch += [dma((3,)), dma((2,)), dma((5, 8)), dma((5, 8)), dma((2, 3)), dma((2, 3))]
    scratch += [dma((len(PEERS_K),))] * 2 + [dma((len(PEERS_G),))] * 2

    def per_device(pressure, inverse_density, source):
        block = jax.ShapeDtypeStruct(pressure.shape, F32)
        return pl.pallas_call(
            functools.partial(kernel, ngx, ngy),
            out_shape=(block, block),
            in_specs=[pl.BlockSpec(memory_space=pl.ANY)] * 3,
            out_specs=[pl.BlockSpec(memory_space=pl.ANY)] * 2,
            scratch_shapes=scratch,
            compiler_params=pltpu.CompilerParams(
                collective_id=0, has_side_effects=True, vmem_limit_bytes=48 * 2**20
            ),
        )(pressure, inverse_density, source)

    spec = P("gx", "gy", None)
    return jax.shard_map(
        per_device, mesh=mesh, in_specs=(spec,) * 3, out_specs=(spec, spec), check_vma=False
    )
```

time: 686 us -> 69.5 us (0.10)
  the two profiles are of different devices: /device:TPU:2 before, /device:TPU:1 now
where the time goes in v1:
time: 69.5 us; the launch traced here: 69.3 us
  Pallas kernels  63.9 us (92%)
  local copies, waits for them, and re-layouts  4.71 us (7%)
    pallas_call x1, Pallas kernels, per_device(): pl.pallas_call(functools.partial(kernel, ngx, ngy), out_shape=(block, blo...  63.9 us
    unnamed x8, local copies, waits for them, and re-layouts  4.71 us

profile of v1, /device:TPU:1, one launch (start us, length us, event | category | flops | bytes accessed | tf_op | source)
XLA Modules:
  0.0 69.3 jit_solution(16864036956927625980)
XLA Ops:
  0.6 0.0 copy-start
  0.6 1.0 %copy-done = f32[16,64,128]{2,1,0:T(8,128)S(1)} copy-done((f32[16,64,128]{2,1,0:T(8,128)S(1)}, f32[16,64,128]{2,1,0:T(8,128)}, u32[]{:S(2)}) %copy-start) | copy-done | bytes 524312
  1.7 0.0 copy-start.1
  1.7 1.0 %copy-done.1 = f32[16,64,128]{2,1,0:T(8,128)S(1)} copy-done((f32[16,64,128]{2,1,0:T(8,128)S(1)}, f32[16,64,128]{2,1,0:T(8,128)}, u32[]{:S(2)}) %copy-start.1) | copy-done | bytes 524312
  2.7 0.0 copy-start.2
  2.7 1.0 %copy-done.2 = f32[16,64,128]{2,1,0:T(8,128)S(1)} copy-done((f32[16,64,128]{2,1,0:T(8,128)S(1)}, f32[16,64,128]{2,1,0:T(8,128)}, u32[]{:S(2)}) %copy-start.2) | copy-done | bytes 524312
  3.8 63.9 %shard_map.50 = (f32[16,64,128]{2,1,0:T(8,128)S(1)}, f32[16,64,128]{2,1,0:T(8,128)S(1)}) custom-call(f32[16,64,128]{2,1,0:T(8,128)S(1)} %copy-done, f32[16,64,128]{2,1,0:T(8,128)S(1)} %copy-done.1, f32[16,64,128]{2,1,0:T(8,128)S(1)} %copy-done.2), custom_call_target="tpu_custom_call" | custom-call | tf_op jit(solution)/shard_map/pallas_call | solution.py:523
  67.7 0.8 %copy.7 = f32[16,64,128]{2,1,0:T(8,128)} copy(f32[16,64,128]{2,1,0:T(8,128)S(1)} %get-tuple-element.4) | data formatting | bytes 1048576
  68.5 0.8 %copy.8 = f32[16,64,128]{2,1,0:T(8,128)} copy(f32[16,64,128]{2,1,0:T(8,128)S(1)} %get-tuple-element.5) | data formatting | bytes 1048576
Async XLA Ops:
  0.6 1.0 %copy-start = (f32[16,64,128]{2,1,0:T(8,128)S(1)}, f32[16,64,128]{2,1,0:T(8,128)}, u32[]{:S(2)}) copy-start(f32[16,64,128]{2,1,0:T(8,128)} %p_hbm.1) | copy-start | bytes 1572868
  1.7 1.0 %copy-start.1 = (f32[16,64,128]{2,1,0:T(8,128)S(1)}, f32[16,64,128]{2,1,0:T(8,128)}, u32[]{:S(2)}) copy-start(f32[16,64,128]{2,1,0:T(8,128)} %k_hbm.1) | copy-start | bytes 1572868
  2.7 1.0 %copy-start.2 = (f32[16,64,128]{2,1,0:T(8,128)S(1)}, f32[16,64,128]{2,1,0:T(8,128)}, u32[]{:S(2)}) copy-start(f32[16,64,128]{2,1,0:T(8,128)} %s_hbm.1) | copy-start | bytes 1572868

commit v2 on v1

--- a/solution.py
+++ b/solution.py
@@ -28,12 +28,23 @@
     return pltpu.roll(x, shift % x.shape[axis], axis)
 
 
-def loop(lo, hi, body):
+def loop(lo, hi, body, most=8):
+    n = hi - lo
+    sizes = [u for u in range(4, most + 1) if n % u == 0]
+    size = max(sizes) if sizes else -(-n // -(-n // most)) - (1 if n > most else 0)
+    turns = n // size
+
     def step(i, carry):
+        for j in range(size):
+            body(lo + i * size + j)
+        return carry
+
+    if turns > 1:
+        lax.fori_loop(0, turns, step, 0)
+    else:
+        step(0, 0)
+    for i in range(lo + turns * size, hi):
         body(i)
-        return carry
-
-    lax.fori_loop(lo, hi, step, 0)
 
 
 def strips(lo, hi, size=16):
@@ -120,7 +131,7 @@
     def gather(j):
         x = plane(j)
         for r, n in rows:
-            tmp[j, pl.ds(r, n), :] = pair_sum_z(value(x, r, n) + value(x + 1, r, n), s)
+            tmp[j, pl.ds(r, n), :] = value(x, r, n) + value(x + 1, r, n)
 
     loop(lo, hi, gather)
     first, count = rows[0][0], sum(n for _, n in rows) // 2
@@ -128,7 +139,7 @@
     def squeeze(j):
         even = tmp[j, pl.ds(first, count, stride=2), :]
         odd = tmp[j, pl.ds(first + 1, count, stride=2), :]
-        dst[j, pl.ds(dst_rows, count), :] = 0.125 * (even + odd)
+        dst[j, pl.ds(dst_rows, count), :] = 0.125 * pair_sum_z(even + odd, s)
 
     loop(lo, hi, squeeze)
 
@@ -251,15 +262,15 @@
     for c in loads:
         c.start()
 
-    greet = list(SIDES) + [(0, 2)] + [(o, 0) for o in PEERS_K if abs(o) > 1]
+    greet = [(o, 0) for o in PEERS_K if abs(o) > 1] + [(0, 2)] + list(SIDES)[::-1]
     barrier = pltpu.get_barrier_semaphore()
     for o in greet:
         pl.semaphore_signal(barrier, inc=1, device_id=peer(*o), device_id_type=MESH)
 
     waits = []
 
-    def exchange(which, src, dst, x0, nx, hx, ny):
-        y0, hy = 16, 8
+    def exchange(which, src, dst, x0, nx, hx, ny, hy):
+        y0 = 16
         lead = (slice(None),) * (len(src.shape) - 3)
         copies = []
         for i, (dx, dy) in enumerate(SIDES):
@@ -310,39 +321,48 @@
     l0 = Level(1, 1.0, coef, r0, fx0, fy0, fz0, wt0, d0)
     l1 = Level(2, 0.25, k1, r1, fx1, fy1, fz1, wt1, d1)
     l2 = Level(4, 0.0625, k2, r2, fx2, fy2, fz2, wt2, d2)
-    all0, own0 = strips(8, 88), strips(16, 80)
+    all0, own0, mid0, rim0 = strips(8, 88), strips(16, 80), strips(24, 72), [(8, 16), (72, 16)]
     all1, own1 = strips(8, 56), strips(16, 48)
     all2 = strips(8, 40)
 
-    loads[0].wait()
+    for c in loads:
+        c.wait()
+    pl.semaphore_wait(barrier, len(greet))
+    a_in = exchange(0, w0, w0, 3, 16, 3, 64, 3)
     coarsen(lambda x, r, n: coef[x, pl.ds(r, n), :], 1, tmp1, k1, (8, 16, lambda j: 2 * j - 13), own0, 16)
     coarsen(lambda x, r, n: k1[x, pl.ds(r, n), :], 2, tmp2, k2, (4, 8, lambda j: 2 * j), own1, 16)
     for p, row in enumerate(pack_rows([k2[4 + i, pl.ds(16, 16), :] for i in range(4)])):
         yk[gy, pl.ds(p, 1), :] = row
-    loads[1].wait()
-    loads[2].wait()
-
-    pl.semaphore_wait(barrier, len(greet))
-    a_in = exchange(0, w0, w0, 3, 16, 3, 64)
-    k1_in = exchange(1, k1, k1, 8, 8, 8, 32)
+    k1_in = exchange(1, k1, k1, 8, 8, 8, 32, 8)
     yk_in = gather_y(0, yk)
 
+    l0.inverses((3, 19), own0)
+    l0.faces((3, 18), own0)
+    l0.diagonal((4, 18), mid0)
+    l0.sweep(press, source, va0, (4, 18), mid0)
+
+    arrive(a_in)
+    for planes in ((0, 3), (19, 22)):
+        l0.inverses(planes, all0)
+    l0.inverses((3, 19), [(8, 8), (80, 8)])
+    for planes in ((0, 3), (18, 21)):
+        l0.faces(planes, all0)
+    l0.faces((3, 18), [(8, 8), (72, 16)])
+    for planes in ((1, 4), (18, 21)):
+        l0.diagonal(planes, all0)
+    l0.diagonal((4, 18), rim0)
+    for planes in ((1, 4), (18, 21)):
+        l0.sweep(press, source, va0, planes, all0)
+    l0.sweep(press, source, va0, (4, 18), rim0)
+    l0.sweep(va0, source, vb0, (2, 20), all0)
+    coarsen(
+        functools.partial(l0.residual, vb0, source), 1, tmp1, g1, (8, 16, lambda j: 2 * j - 13), own0, 16
+    )
+    g1_in = exchange(2, g1, g1, 8, 8, 6, 32, 8)
     arrive(yk_in)
     for i in range(4):
         xk[pl.ds(8 * REACH_K + 2 * i, 2), :] = yk[i, pl.ds(0, 2), :]
     xk_in = gather_x(xk, PEERS_K, xk_s, xk_r)
-
-    arrive(a_in)
-    l0.inverses((0, 22), all0)
-    l0.faces((0, 21), all0)
-    l0.diagonal((1, 21), all0)
-    l0.sweep(press, source, va0, (1, 21), all0)
-    l0.sweep(va0, source, vb0, (2, 20), all0)
-    coarsen(
-        functools.partial(l0.residual, vb0, source), 1, tmp1, g1, (8, 16, lambda j: 2 * j - 13), own0, 16
-    )
-    g1_in = exchange(2, g1, g1, 8, 8, 6, 32)
-    v0_in = exchange(3, vb0, vs0, 3, 16, 3, 64)
 
     arrive(k1_in)
     l1.inverses((0, 24), all1)
@@ -359,30 +379,8 @@
 
     loop(3, 19, keep)
 
-    arrive(xk_in)
-    shape = (SLOTS, LANES)
-    pack3, pack4 = Packed3(shape), Packed4(shape)
-    kk = [xk[pl.ds(i, SLOTS, stride=8), :] for i in range(8)]
-    f, d = packed_coefs(pack3, kk, 1.0 / 64)
-    for i in range(8):
-        for j, value in enumerate((f[0][i], f[1][i], f[2][i], OMEGA * recip(d[i]), d[i])):
-            c3[j, i] = value
-    l, t = grid2((LANES, LANES))
-
-    def squeeze(values):
-        out = None
-        for i in range(4):
-            y = t // 8 - 4 * i
-            choose = jnp.where((l // 32 == y) & ((l % 16) // 2 == t % 8), 0.125, 0.0).astype(F32)
-            part = dot(values[2 * i] + values[2 * i + 1], choose)
-            out = part if out is None else out + part
-        return out
-
-    f, d = packed_coefs(pack4, [squeeze(kk)], 1.0 / 256)
-    for j, value in enumerate((f[0][0], f[1][0], f[2][0], OMEGA * recip(d[0]))):
-        c4[j] = value
-
     arrive(g1_in)
+    v0_in = exchange(3, vb0, vs0, 3, 16, 3, 64, 3)
     l1.first_sweep(g1, va1, (2, 22), all1)
     l1.sweep(va1, g1, vb1, (3, 21), all1)
     coarsen(
@@ -397,7 +395,30 @@
     for x in range(4, 8):
         w2[0, x, pl.ds(16, 16), :] = vb2[x, pl.ds(16, 16), :]
         w2[1, x, pl.ds(16, 16), :] = g2[x, pl.ds(16, 16), :]
-    w2_in = exchange(4, w2, w2, 4, 4, 4, 16)
+    w2_in = exchange(4, w2, w2, 4, 4, 4, 16, 8)
+    arrive(xk_in)
+    shape = (SLOTS, LANES)
+    pack3, pack4 = Packed3(shape), Packed4(shape)
+    kk = [xk[pl.ds(i, SLOTS, stride=8), :] for i in range(8)]
+    f, d = packed_coefs(pack3, kk, 1.0 / 64)
+    for i in range(8):
+        for j, value in enumerate((f[0][i], f[1][i], f[2][i], OMEGA * recip(d[i]), d[i])):
+            c3[j, i] = value
+    l, t = grid2((LANES, LANES))
+
+    def squeeze(values):
+        out = None
+        for i in range(4):
+            y = t // 8 - 4 * i
+            choose = jnp.where((l // 32 == y) & ((l % 16) // 2 == t % 8), 0.125, 0.0).astype(F32)
+            part = dot(values[2 * i] + values[2 * i + 1], choose)
+            out = part if out is None else out + part
+        return out
+
+    f, d = packed_coefs(pack4, [squeeze(kk)], 1.0 / 256)
+    for j, value in enumerate((f[0][0], f[1][0], f[2][0], OMEGA * recip(d[0]))):
+        c4[j] = value
+
     arrive(yg_in)
     for i in range(4):
         xg[pl.ds(8 * REACH_K + 2 * i, 2), :] = yg[i, pl.ds(0, 2), :]
@@ -523,11 +544,11 @@
         return pl.pallas_call(
             functools.partial(kernel, ngx, ngy),
             out_shape=(block, block),
-            in_specs=[pl.BlockSpec(memory_space=pl.ANY)] * 3,
+            in_specs=[pl.BlockSpec(memory_space=pltpu.HBM)] * 3,
             out_specs=[pl.BlockSpec(memory_space=pl.ANY)] * 2,
             scratch_shapes=scratch,
             compiler_params=pltpu.CompilerParams(
-                collective_id=0, has_side_effects=True, vmem_limit_bytes=48 * 2**20
+                collective_id=0, has_side_effects=True, vmem_limit_bytes=105 * 2**19
             ),
         )(pressure, inverse_density, source)
 

time: 69.5 us -> 44.6 us (0.64)
  Pallas kernels: 63.9 us -> 42.2 us
  local copies, waits for them, and re-layouts: 4.71 us -> 1.59 us
    pallas_call x1, Pallas kernels: 63.9 us -> 42.2 us  [per_device(): pl.pallas_call(functools.partial(kernel, ngx, ngy), out_shape=(block, blo...]
    unnamed x8 -> x2, local copies, waits for them, and re-layouts: 4.71 us -> 1.59 us
where the time goes in v2:
time: 44.6 us; the launch traced here: 44.5 us
  Pallas kernels  42.2 us (95%)
  local copies, waits for them, and re-layouts  1.59 us (4%)
  between operations  0.64 us (1%)
    pallas_call x1, Pallas kernels, per_device(): pl.pallas_call(functools.partial(kernel, ngx, ngy), out_shape=(block, blo...  42.2 us
    unnamed x2, local copies, waits for them, and re-layouts  1.59 us

profile of v2, /device:TPU:1, one launch (start us, length us, event | category | flops | bytes accessed | tf_op | source)
XLA Modules:
  0.0 44.5 jit_solution(2950648070146794531)
XLA Ops:
  0.6 42.2 %shard_map.50 = (f32[16,64,128]{2,1,0:T(8,128)S(1)}, f32[16,64,128]{2,1,0:T(8,128)S(1)}) custom-call(f32[16,64,128]{2,1,0:T(8,128)} %p_hbm.1, f32[16,64,128]{2,1,0:T(8,128)} %k_hbm.1, f32[16,64,128]{2,1,0:T(8,128)} %s_hbm.1), custom_call_target="tpu_custom_call" | custom-call | tf_op jit(solution)/shard_map/pallas_call | solution.py:544
  42.9 0.8 %copy.7 = f32[16,64,128]{2,1,0:T(8,128)} copy(f32[16,64,128]{2,1,0:T(8,128)S(1)} %get-tuple-element.4) | data formatting | bytes 1048576
  43.7 0.8 %copy.8 = f32[16,64,128]{2,1,0:T(8,128)} copy(f32[16,64,128]{2,1,0:T(8,128)S(1)} %get-tuple-element.5) | data formatting | bytes 1048576

commit v3 on v2

--- a/solution.py
+++ b/solution.py
@@ -9,14 +9,12 @@
 
 MESH = pl.DeviceIdType.MESH
 F32 = jnp.float32
+BF16 = jnp.bfloat16
 OMEGA = 0.8
 LANES = 128
 SIDES = ((-1, 0), (1, 0), (0, -1), (0, 1), (-1, -1), (-1, 1), (1, -1), (1, 1))
-REACH_G = 10
-REACH_K = 11
 SLOTS = 24
-PEERS_K = [o for d in range(REACH_K, 0, -1) for o in (d, -d)]
-PEERS_G = [o for d in range(REACH_G, 0, -1) for o in (d, -d)]
+CHIPS = [c for d in range(5, 0, -1) for c in (d, -d)]
 
 
 def recip(x):
@@ -125,7 +123,7 @@
         return g[x, pl.ds(r, n), :] + a - self.d[x, pl.ds(r, n), :] * here
 
 
-def coarsen(value, s, tmp, dst, pairs, rows, dst_rows):
+def add_planes(value, tmp, pairs, rows):
     lo, hi, plane = pairs
 
     def gather(j):
@@ -134,6 +132,12 @@
             tmp[j, pl.ds(r, n), :] = value(x, r, n) + value(x + 1, r, n)
 
     loop(lo, hi, gather)
+
+
+def coarsen(value, s, tmp, dst, pairs, rows, dst_rows, parts=None):
+    lo, hi, plane = pairs
+    for part_lo, part_hi, part_rows in parts or [(lo, hi, rows)]:
+        add_planes(value, tmp, (part_lo, part_hi, plane), part_rows)
     first, count = rows[0][0], sum(n for _, n in rows) // 2
 
     def squeeze(j):
@@ -222,8 +226,14 @@
     ]
 
 
-def dot(a, b):
-    return jnp.dot(a, b, precision=lax.Precision.HIGHEST, preferred_element_type=F32)
+def dot(a, choose):
+    out = None
+    for _ in range(3):
+        part = a.astype(BF16)
+        a = a - part.astype(F32)
+        term = jnp.dot(part, choose, preferred_element_type=F32)
+        out = term if out is None else out + term
+    return out
 
 
 def grid2(shape):
@@ -232,7 +242,7 @@
 
 def pack_rows(cells):
     l, t = grid2((LANES, LANES))
-    choose = jnp.where((l // 8 == t % 16) & (l % 4 == 0), 0.125, 0.0).astype(F32)
+    choose = jnp.where((l // 8 == t % 16) & (l % 4 == 0), 0.125, 0.0).astype(BF16)
     r, t = grid2((16, LANES))
     keep = r // 2 == t // 16
     rows = []
@@ -247,10 +257,11 @@
     w0, r0, fx0, fy0, fz0, wt0, d0, va0, vb0, vs0, res0,
     k1, r1, fx1, fy1, fz1, wt1, d1, g1, va1, vb1, dup1,
     k2, r2, fx2, fy2, fz2, wt2, d2, g2, va2, vb2, w2, dup2,
-    tmp1, tmp2, yk, yg, xk, xg, c3, c4, v3,
-    load_sem, store_sem, side_s, side_r, y_s, y_r, xk_s, xk_r, xg_s, xg_r,
+    tmp1, tmp2, tmp0, yk, yg, xk, xg, c3, c4, v3,
+    load_sem, store_sem, side_s, side_r, gather_sem,
 ):
     gx, gy = lax.axis_index("gx"), lax.axis_index("gy")
+    parity = lax.rem(gx, 2)
 
     def peer(dx, dy):
         return (lax.rem(gx + (dx + ngx), ngx), lax.rem(gy + (dy + ngy), ngy))
@@ -262,7 +273,7 @@
     for c in loads:
         c.start()
 
-    greet = [(o, 0) for o in PEERS_K if abs(o) > 1] + [(0, 2)] + list(SIDES)[::-1]
+    greet = [(2 * c, 0) for c in (6, -6, *CHIPS)] + [(0, 2), (1 - 2 * parity, 2)] + list(SIDES)[::-1]
     barrier = pltpu.get_barrier_semaphore()
     for o in greet:
         pl.semaphore_signal(barrier, inc=1, device_id=peer(*o), device_id_type=MESH)
@@ -287,35 +298,52 @@
         waits.extend(copies)
         return copies
 
-    def gather_y(which, buf):
-        copies = []
-        for o in (1, 2, 3):
+    def wait_all(buf, tiles, send, recv):
+        every = buf.at[pl.ds(0, 8 * tiles), :]
+        c = pltpu.make_async_remote_copy(
+            src_ref=every, dst_ref=every, send_sem=send, recv_sem=recv,
+            device_id=peer(1, 0), device_id_type=MESH,
+        )
+        waits.append(c)
+        return [c]
+
+    def gather_near(buf, send, recv):
+        mine = pl.ds(pl.multiple_of(8 * (4 * parity + gy), 8), 8)
+        for dx, dy in ((1, 2), (0, 2), (1, 1), (1, 3), (0, 1), (0, 3), (1, 0)):
             c = pltpu.make_async_remote_copy(
-                src_ref=buf.at[gy], dst_ref=buf.at[gy],
-                send_sem=y_s.at[which, o - 1], recv_sem=y_r.at[which, o - 1],
-                device_id=peer(0, o), device_id_type=MESH,
+                src_ref=buf.at[mine, :], dst_ref=buf.at[mine, :], send_sem=send, recv_sem=recv,
+                device_id=peer(dx * (1 - 2 * parity), dy), device_id_type=MESH,
             )
             c.start()
-            copies.append(c)
-        waits.extend(copies)
-        return copies
-
-    def gather_x(buf, peers, send, recv):
-        copies = []
-        for i, o in enumerate(peers):
-            c = pltpu.make_async_remote_copy(
-                src_ref=buf.at[pl.ds(8 * REACH_K, 8), :], dst_ref=buf.at[pl.ds(8 * (REACH_K - o), 8), :],
-                send_sem=send.at[i], recv_sem=recv.at[i],
-                device_id=peer(o, 0), device_id_type=MESH,
+        return wait_all(buf, 7, send, recv)
+
+    def chip_rows(c):
+        return pl.ds(pl.multiple_of(16 * (6 + c - parity), 16), 16)
+
+    def gather_x(buf, chips, send, recv):
+        for c in chips:
+            copy = pltpu.make_async_remote_copy(
+                src_ref=buf.at[chip_rows(0), :], dst_ref=buf.at[chip_rows(-c), :], send_sem=send, recv_sem=recv,
+                device_id=peer(2 * c, 0), device_id_type=MESH,
             )
-            c.start()
-            copies.append(c)
-        waits.extend(copies)
-        return copies
+            copy.start()
+        return wait_all(buf, 2 * len(chips), send, recv)
+
+    def assemble(near, buf):
+        for device in range(2):
+            for i in range(4):
+                row = pl.multiple_of(8 * (2 * (6 - parity) + device), 8) + 2 * i
+                buf[pl.ds(row, 2), :] = near[pl.ds(8 * (4 * device + i), 2), :]
 
     def arrive(copies):
         for c in copies:
             c.wait_recv()
+
+    def sent(keep=0):
+        count = len(waits) - keep
+        for c in waits[:count]:
+            c.wait_send()
+        del waits[:count]
 
     press, coef, source = w0.at[0], w0.at[1], w0.at[2]
     l0 = Level(1, 1.0, coef, r0, fx0, fy0, fz0, wt0, d0)
@@ -328,20 +356,25 @@
     for c in loads:
         c.wait()
     pl.semaphore_wait(barrier, len(greet))
-    a_in = exchange(0, w0, w0, 3, 16, 3, 64, 3)
+    coef_in = exchange(0, coef, coef, 3, 16, 3, 64, 3)
+    press_in = exchange(5, press, press, 3, 16, 3, 64, 3)
+    source_in = exchange(6, source, source, 3, 16, 2, 64, 2)
     coarsen(lambda x, r, n: coef[x, pl.ds(r, n), :], 1, tmp1, k1, (8, 16, lambda j: 2 * j - 13), own0, 16)
     coarsen(lambda x, r, n: k1[x, pl.ds(r, n), :], 2, tmp2, k2, (4, 8, lambda j: 2 * j), own1, 16)
     for p, row in enumerate(pack_rows([k2[4 + i, pl.ds(16, 16), :] for i in range(4)])):
-        yk[gy, pl.ds(p, 1), :] = row
+        yk[pl.ds(8 * (4 * parity + gy) + p, 1), :] = row
     k1_in = exchange(1, k1, k1, 8, 8, 8, 32, 8)
-    yk_in = gather_y(0, yk)
+    yk_in = gather_near(yk, gather_sem.at[0], gather_sem.at[1])
 
     l0.inverses((3, 19), own0)
     l0.faces((3, 18), own0)
-    l0.diagonal((4, 18), mid0)
-    l0.sweep(press, source, va0, (4, 18), mid0)
-
-    arrive(a_in)
+    l0.diagonal((4, 18), own0)
+    l0.sweep(press, source, va0, (4, 18), [(17, 7), *mid0, (72, 7)])
+    l0.sweep(va0, source, vb0, (5, 17), mid0)
+    residual0 = functools.partial(l0.residual, vb0, source)
+    add_planes(residual0, tmp0, (10, 14, lambda j: 2 * j - 13), strips(32, 64))
+
+    arrive(coef_in)
     for planes in ((0, 3), (19, 22)):
         l0.inverses(planes, all0)
     l0.inverses((3, 19), [(8, 8), (80, 8)])
@@ -351,18 +384,23 @@
     for planes in ((1, 4), (18, 21)):
         l0.diagonal(planes, all0)
     l0.diagonal((4, 18), rim0)
+    arrive(press_in)
+    arrive(source_in)
     for planes in ((1, 4), (18, 21)):
         l0.sweep(press, source, va0, planes, all0)
     l0.sweep(press, source, va0, (4, 18), rim0)
-    l0.sweep(va0, source, vb0, (2, 20), all0)
+    for planes in ((2, 5), (17, 20)):
+        l0.sweep(va0, source, vb0, planes, all0)
+    l0.sweep(va0, source, vb0, (5, 17), rim0)
+    edge0 = [(16, 16), (64, 16)]
     coarsen(
-        functools.partial(l0.residual, vb0, source), 1, tmp1, g1, (8, 16, lambda j: 2 * j - 13), own0, 16
+        residual0, 1, tmp0, g1, (8, 16, lambda j: 2 * j - 13), own0, 16,
+        [(8, 10, own0), (10, 14, edge0), (14, 16, own0)],
     )
     g1_in = exchange(2, g1, g1, 8, 8, 6, 32, 8)
     arrive(yk_in)
-    for i in range(4):
-        xk[pl.ds(8 * REACH_K + 2 * i, 2), :] = yk[i, pl.ds(0, 2), :]
-    xk_in = gather_x(xk, PEERS_K, xk_s, xk_r)
+    assemble(yk, xk)
+    xk_in = gather_x(xk, [6 - 12 * parity, *CHIPS], gather_sem.at[4], gather_sem.at[5])
 
     arrive(k1_in)
     l1.inverses((0, 24), all1)
@@ -390,8 +428,8 @@
     l2.sweep(va2, g2, vb2, (3, 9), all2)
     cells = [l2.residual(vb2, g2, 4 + i, 16, 16) for i in range(4)]
     for p, row in enumerate(pack_rows(cells)):
-        yg[gy, pl.ds(p, 1), :] = row
-    yg_in = gather_y(1, yg)
+        yg[pl.ds(8 * (4 * parity + gy) + p, 1), :] = row
+    yg_in = gather_near(yg, gather_sem.at[2], gather_sem.at[3])
     for x in range(4, 8):
         w2[0, x, pl.ds(16, 16), :] = vb2[x, pl.ds(16, 16), :]
         w2[1, x, pl.ds(16, 16), :] = g2[x, pl.ds(16, 16), :]
@@ -410,19 +448,23 @@
         out = None
         for i in range(4):
             y = t // 8 - 4 * i
-            choose = jnp.where((l // 32 == y) & ((l % 16) // 2 == t % 8), 0.125, 0.0).astype(F32)
+            choose = jnp.where((l // 32 == y) & ((l % 16) // 2 == t % 8), 0.125, 0.0).astype(BF16)
             part = dot(values[2 * i] + values[2 * i + 1], choose)
             out = part if out is None else out + part
         return out
 
     f, d = packed_coefs(pack4, [squeeze(kk)], 1.0 / 256)
-    for j, value in enumerate((f[0][0], f[1][0], f[2][0], OMEGA * recip(d[0]))):
+    weight = OMEGA * recip(d[0])
+    faces4 = [weight]
+    for axis, prv in enumerate((pack4.x_prev, pack4.y_prev, pack4.z_prev)):
+        faces4 += [weight * f[axis][0], weight * prv(f[axis])[0]]
+    for j, value in enumerate(faces4):
         c4[j] = value
 
     arrive(yg_in)
-    for i in range(4):
-        xg[pl.ds(8 * REACH_K + 2 * i, 2), :] = yg[i, pl.ds(0, 2), :]
-    xg_in = gather_x(xg, PEERS_G, xg_s, xg_r)
+    assemble(yg, xg)
+    xg_in = gather_x(xg, CHIPS, gather_sem.at[6], gather_sem.at[7])
+    sent(1)
     arrive(xg_in)
 
     g3 = [xg[pl.ds(i, SLOTS, stride=8), :] for i in range(8)]
@@ -432,16 +474,20 @@
     saved = packed_sweep(pack3, f3, wt3, saved, g3)
     around = pack3.both(f3, saved)
     g4 = squeeze([g3[i] + around[i] - c3[4, i] * saved[i] for i in range(8)])
-    f4, wt4 = [[c4[j]] for j in range(3)], [c4[3]]
+    f4 = [c4[j] for j in range(7)]
+    start = f4[0] * g4
 
     def coarsest(_, v):
-        return packed_sweep(pack4, f4, wt4, [v], [g4])[0]
-
-    v4 = lax.fori_loop(0, 7, coarsest, wt4[0] * g4)
+        a = f4[1] * pack4.x_next([v])[0] + f4[2] * pack4.x_prev([v])[0]
+        b = f4[3] * pack4.y_next([v])[0] + f4[4] * pack4.y_prev([v])[0]
+        c = f4[5] * pack4.z_next([v])[0] + f4[6] * pack4.z_prev([v])[0]
+        return ((1.0 - OMEGA) * v + start) + (a + b) + c
+
+    v4 = lax.fori_loop(0, 7, coarsest, start)
     v = []
     for i in range(4):
         y = l // 8 - 4 * i
-        spread = jnp.where((t // 32 == y) & ((t % 16) // 2 == l % 8), 1.0, 0.0).astype(F32)
+        spread = jnp.where((t // 32 == y) & ((t % 16) // 2 == l % 8), 1.0, 0.0).astype(BF16)
         part = dot(v4, spread)
         v += [saved[2 * i] + part, saved[2 * i + 1] + part]
     for _ in range(2):
@@ -454,11 +500,12 @@
     high = lax.rem(gy + 1, ngy)
     parts = []
     for j in range(6):
-        slot, p = REACH_K - 1 + j // 2, j % 2
+        slot, p = 10 + j // 2, j % 2
         for part, y in ((low, 4), (gy, 0), (gy, 4), (high, 0)):
-            row = jnp.broadcast_to(v3[2 * part + p, pl.ds(slot, 1), :], (8, LANES))
+            rows = [v3[2 * part + p, pl.ds(slot + i, 1), :] for i in range(2)]
+            row = jnp.broadcast_to(jnp.where(parity == 1, rows[0], rows[1]), (8, LANES))
             parts.append(jnp.where(t8 // 16 == r // 2 + y, row, 0.0))
-    spread = jnp.where(l % 16 == t // 8, 1.0, 0.0).astype(F32)
+    spread = jnp.where(l % 16 == t // 8, 1.0, 0.0).astype(BF16)
     fine = dot(jnp.concatenate(parts, axis=0), spread)
     for j in range(6):
         dup2[j] = fine[32 * j : 32 * j + 32]
@@ -494,8 +541,6 @@
 
     loop(6, 18, double1)
     arrive(v0_in)
-    for c in v0_in:
-        c.wait_send()
 
     def correct0(x):
         for r, n in all0:
@@ -514,10 +559,7 @@
     loop(3, 19, final)
     r_store = pltpu.make_async_copy(res0, r_out, store_sem.at[1])
     r_store.start()
-    done = [id(c) for c in v0_in]
-    for c in waits:
-        if id(c) not in done:
-            c.wait_send()
+    sent()
     v_store.wait()
     r_store.wait()
 
@@ -532,12 +574,11 @@
     scratch = [vmem(3, *n0)] + [vmem(*n0)] * 9 + [vmem(16, 64, LANES)]
     scratch += [vmem(*n1)] * 10 + [vmem(12, 64, LANES)]
     scratch += [vmem(*n2)] * 10 + [vmem(2, *n2), vmem(6, 32, LANES)]
-    scratch += [vmem(18, 96, LANES), vmem(12, 64, LANES)]
-    scratch += [vmem(4, 8, LANES)] * 2 + [vmem(8 * SLOTS, LANES)] * 2
-    scratch += [vmem(5, 8, SLOTS, LANES), vmem(4, SLOTS, LANES), vmem(8, SLOTS, LANES)]
+    scratch += [vmem(18, 96, LANES), vmem(12, 64, LANES), vmem(16, 96, LANES)]
+    scratch += [vmem(64, LANES)] * 2 + [vmem(8 * SLOTS, LANES)] * 2
+    scratch += [vmem(5, 8, SLOTS, LANES), vmem(7, SLOTS, LANES), vmem(8, SLOTS, LANES)]
     dma = pltpu.SemaphoreType.DMA
-    scratch += [dma((3,)), dma((2,)), dma((5, 8)), dma((5, 8)), dma((2, 3)), dma((2, 3))]
-    scratch += [dma((len(PEERS_K),))] * 2 + [dma((len(PEERS_G),))] * 2
+    scratch += [dma((3,)), dma((2,)), dma((7, 8)), dma((7, 8)), dma((8,))]
 
     def per_device(pressure, inverse_density, source):
         block = jax.ShapeDtypeStruct(pressure.shape, F32)

time: 44.6 us -> 41.9 us (0.939)
  Pallas kernels: 42.2 us -> 39.6 us
    pallas_call x1, Pallas kernels: 42.2 us -> 39.6 us  [per_device(): pl.pallas_call(functools.partial(kernel, ngx, ngy), out_shape=(block, blo...]
where the time goes in v3:
time: 41.9 us; the launch traced here: 41.8 us
  Pallas kernels  39.6 us (95%)
  local copies, waits for them, and re-layouts  1.59 us (4%)
  between operations  0.64 us (2%)
    pallas_call x1, Pallas kernels, per_device(): pl.pallas_call(functools.partial(kernel, ngx, ngy), out_shape=(block, blo...  39.6 us
    unnamed x2, local copies, waits for them, and re-layouts  1.59 us

profile of v3, /device:TPU:1, one launch (start us, length us, event | category | flops | bytes accessed | tf_op | source)
XLA Modules:
  0.0 41.8 jit_solution(5200897197180668025)
XLA Ops:
  0.6 39.6 %shard_map.50 = (f32[16,64,128]{2,1,0:T(8,128)S(1)}, f32[16,64,128]{2,1,0:T(8,128)S(1)}) custom-call(f32[16,64,128]{2,1,0:T(8,128)} %p_hbm.1, f32[16,64,128]{2,1,0:T(8,128)} %k_hbm.1, f32[16,64,128]{2,1,0:T(8,128)} %s_hbm.1), custom_call_target="tpu_custom_call" | custom-call | tf_op jit(solution)/shard_map/pallas_call | solution.py:585
  40.2 0.8 %copy.7 = f32[16,64,128]{2,1,0:T(8,128)} copy(f32[16,64,128]{2,1,0:T(8,128)S(1)} %get-tuple-element.4) | data formatting | bytes 1048576
  41.0 0.8 %copy.8 = f32[16,64,128]{2,1,0:T(8,128)} copy(f32[16,64,128]{2,1,0:T(8,128)S(1)} %get-tuple-element.5) | data formatting | bytes 1048576

commit v4 on v3

--- a/solution.py
+++ b/solution.py
@@ -26,23 +26,12 @@
     return pltpu.roll(x, shift % x.shape[axis], axis)
 
 
-def loop(lo, hi, body, most=8):
-    n = hi - lo
-    sizes = [u for u in range(4, most + 1) if n % u == 0]
-    size = max(sizes) if sizes else -(-n // -(-n // most)) - (1 if n > most else 0)
-    turns = n // size
-
+def loop(lo, hi, body):
     def step(i, carry):
-        for j in range(size):
-            body(lo + i * size + j)
+        body(i)
         return carry
 
-    if turns > 1:
-        lax.fori_loop(0, turns, step, 0)
-    else:
-        step(0, 0)
-    for i in range(lo + turns * size, hi):
-        body(i)
+    lax.fori_loop(lo, hi, step, 0, unroll=hi - lo)
 
 
 def strips(lo, hi, size=16):
@@ -556,12 +545,15 @@
         for r, n in own0:
             res0[x - 3, pl.ds(r - 16, n), :] = l0.residual(va0, source, x, r, n)
 
-    loop(3, 19, final)
-    r_store = pltpu.make_async_copy(res0, r_out, store_sem.at[1])
-    r_store.start()
+    stores = [v_store]
+    for half in range(2):
+        loop(3 + 8 * half, 11 + 8 * half, final)
+        planes = pl.ds(8 * half, 8)
+        stores.append(pltpu.make_async_copy(res0.at[planes], r_out.at[planes], store_sem.at[1 + half]))
+        stores[-1].start()
     sent()
-    v_store.wait()
-    r_store.wait()
+    for c in stores:
+        c.wait()
 
 
 def solution(mesh):
@@ -578,7 +570,7 @@
     scratch += [vmem(64, LANES)] * 2 + [vmem(8 * SLOTS, LANES)] * 2
     scratch += [vmem(5, 8, SLOTS, LANES), vmem(7, SLOTS, LANES), vmem(8, SLOTS, LANES)]
     dma = pltpu.SemaphoreType.DMA
-    scratch += [dma((3,)), dma((2,)), dma((7, 8)), dma((7, 8)), dma((8,))]
+    scratch += [dma((3,)), dma((3,)), dma((7, 8)), dma((7, 8)), dma((8,))]
 
     def per_device(pressure, inverse_density, source):
         block = jax.ShapeDtypeStruct(pressure.shape, F32)

time: 41.9 us -> 40.5 us (0.967)
  Pallas kernels: 39.6 us -> 38.1 us
    pallas_call x1, Pallas kernels: 39.6 us -> 38.1 us  [per_device(): pl.pallas_call(functools.partial(kernel, ngx, ngy), out_shape=(block, blo...]
where the time goes in v4:
time: 40.5 us; the launch traced here: 40.4 us
  Pallas kernels  38.1 us (94%)
  local copies, waits for them, and re-layouts  1.59 us (4%)
  between operations  0.64 us (2%)
    pallas_call x1, Pallas kernels, per_device(): pl.pallas_call(functools.partial(kernel, ngx, ngy), out_shape=(block, blo...  38.1 us
    unnamed x2, local copies, waits for them, and re-layouts  1.59 us

profile of v4, /device:TPU:1, one launch (start us, length us, event | category | flops | bytes accessed | tf_op | source)
XLA Modules:
  0.0 40.4 jit_solution(6026874566507470928)
XLA Ops:
  0.6 38.1 %shard_map.50 = (f32[16,64,128]{2,1,0:T(8,128)S(1)}, f32[16,64,128]{2,1,0:T(8,128)S(1)}) custom-call(f32[16,64,128]{2,1,0:T(8,128)} %p_hbm.1, f32[16,64,128]{2,1,0:T(8,128)} %k_hbm.1, f32[16,64,128]{2,1,0:T(8,128)} %s_hbm.1), custom_call_target="tpu_custom_call" | custom-call | tf_op jit(solution)/shard_map/pallas_call | solution.py:577
  38.8 0.8 %copy.7 = f32[16,64,128]{2,1,0:T(8,128)} copy(f32[16,64,128]{2,1,0:T(8,128)S(1)} %get-tuple-element.4) | data formatting | bytes 1048576
  39.6 0.8 %copy.8 = f32[16,64,128]{2,1,0:T(8,128)} copy(f32[16,64,128]{2,1,0:T(8,128)S(1)} %get-tuple-element.5) | data formatting | bytes 1048576

commit v5 on v4

--- a/solution.py
+++ b/solution.py
@@ -244,7 +244,7 @@
 def kernel(
     ngx, ngy, p_hbm, k_hbm, s_hbm, v_out, r_out,
     w0, r0, fx0, fy0, fz0, wt0, d0, va0, vb0, vs0, res0,
-    k1, r1, fx1, fy1, fz1, wt1, d1, g1, va1, vb1, dup1,
+    k1, r1, fx1, fy1, fz1, wt1, d1, g1, va1, vb1, dup1, pk1,
     k2, r2, fx2, fy2, fz2, wt2, d2, g2, va2, vb2, w2, dup2,
     tmp1, tmp2, tmp0, yk, yg, xk, xg, c3, c4, v3,
     load_sem, store_sem, side_s, side_r, gather_sem,
@@ -386,7 +386,13 @@
         residual0, 1, tmp0, g1, (8, 16, lambda j: 2 * j - 13), own0, 16,
         [(8, 10, own0), (10, 14, edge0), (14, 16, own0)],
     )
-    g1_in = exchange(2, g1, g1, 8, 8, 6, 32, 8)
+    even = lane_index((48, LANES)) % 2 == 0
+
+    def pack(q):
+        pk1[q, pl.ds(16, 32), :] = jnp.where(even[:32], g1[2 * q, pl.ds(16, 32), :], g1[2 * q + 1, pl.ds(16, 32), :])
+
+    loop(4, 8, pack)
+    g1_in = exchange(2, pk1, pk1, 4, 4, 3, 32, 8)
     arrive(yk_in)
     assemble(yk, xk)
     xk_in = gather_x(xk, [6 - 12 * parity, *CHIPS], gather_sem.at[4], gather_sem.at[5])
@@ -407,6 +413,13 @@
     loop(3, 19, keep)
 
     arrive(g1_in)
+
+    def unpack(q):
+        both = pk1[q, pl.ds(8, 48), :]
+        g1[2 * q, pl.ds(8, 48), :] = jnp.where(even, both, roll(both, 1, 1))
+        g1[2 * q + 1, pl.ds(8, 48), :] = jnp.where(even, roll(both, -1, 1), both)
+
+    loop(1, 11, unpack)
     v0_in = exchange(3, vb0, vs0, 3, 16, 3, 64, 3)
     l1.first_sweep(g1, va1, (2, 22), all1)
     l1.sweep(va1, g1, vb1, (3, 21), all1)
@@ -564,7 +577,7 @@
 
     n0, n1, n2 = (22, 96, LANES), (24, 64, LANES), (12, 48, LANES)
     scratch = [vmem(3, *n0)] + [vmem(*n0)] * 9 + [vmem(16, 64, LANES)]
-    scratch += [vmem(*n1)] * 10 + [vmem(12, 64, LANES)]
+    scratch += [vmem(*n1)] * 10 + [vmem(12, 64, LANES)] * 2
     scratch += [vmem(*n2)] * 10 + [vmem(2, *n2), vmem(6, 32, LANES)]
     scratch += [vmem(18, 96, LANES), vmem(12, 64, LANES), vmem(16, 96, LANES)]
     scratch += [vmem(64, LANES)] * 2 + [vmem(8 * SLOTS, LANES)] * 2

time: 40.5 us -> 39.7 us (0.980)
  Pallas kernels: 38.1 us -> 37.4 us
    pallas_call x1, Pallas kernels: 38.1 us -> 37.4 us  [per_device(): pl.pallas_call(functools.partial(kernel, ngx, ngy), out_shape=(block, blo...]
where the time goes in v5:
time: 39.7 us; the launch traced here: 39.6 us
  Pallas kernels  37.4 us (94%)
  local copies, waits for them, and re-layouts  1.59 us (4%)
  between operations  0.64 us (2%)
    pallas_call x1, Pallas kernels, per_device(): pl.pallas_call(functools.partial(kernel, ngx, ngy), out_shape=(block, blo...  37.4 us
    unnamed x2, local copies, waits for them, and re-layouts  1.59 us

profile of v5, /device:TPU:1, one launch (start us, length us, event | category | flops | bytes accessed | tf_op | source)
XLA Modules:
  0.0 39.6 jit_solution(4516555608886990086)
XLA Ops:
  0.6 37.4 %shard_map.50 = (f32[16,64,128]{2,1,0:T(8,128)S(1)}, f32[16,64,128]{2,1,0:T(8,128)S(1)}) custom-call(f32[16,64,128]{2,1,0:T(8,128)} %p_hbm.1, f32[16,64,128]{2,1,0:T(8,128)} %k_hbm.1, f32[16,64,128]{2,1,0:T(8,128)} %s_hbm.1), custom_call_target="tpu_custom_call" | custom-call | tf_op jit(solution)/shard_map/pallas_call | solution.py:590
  38.1 0.8 %copy.7 = f32[16,64,128]{2,1,0:T(8,128)} copy(f32[16,64,128]{2,1,0:T(8,128)S(1)} %get-tuple-element.4) | data formatting | bytes 1048576
  38.8 0.8 %copy.8 = f32[16,64,128]{2,1,0:T(8,128)} copy(f32[16,64,128]{2,1,0:T(8,128)S(1)} %get-tuple-element.5) | data formatting | bytes 1048576

commit v6 on v5

--- a/solution.py
+++ b/solution.py
@@ -245,7 +245,7 @@
     ngx, ngy, p_hbm, k_hbm, s_hbm, v_out, r_out,
     w0, r0, fx0, fy0, fz0, wt0, d0, va0, vb0, vs0, res0,
     k1, r1, fx1, fy1, fz1, wt1, d1, g1, va1, vb1, dup1, pk1,
-    k2, r2, fx2, fy2, fz2, wt2, d2, g2, va2, vb2, w2, dup2,
+    k2, r2, fx2, fy2, fz2, wt2, d2, g2, va2, vb2, w2, pk2, dup2,
     tmp1, tmp2, tmp0, yk, yg, xk, xg, c3, c4, v3,
     load_sem, store_sem, side_s, side_r, gather_sem,
 ):
@@ -412,16 +412,23 @@
 
     loop(3, 19, keep)
 
+    l1.first_sweep(g1, va1, (8, 16), own1)
     arrive(g1_in)
 
-    def unpack(q):
-        both = pk1[q, pl.ds(8, 48), :]
-        g1[2 * q, pl.ds(8, 48), :] = jnp.where(even, both, roll(both, 1, 1))
-        g1[2 * q + 1, pl.ds(8, 48), :] = jnp.where(even, roll(both, -1, 1), both)
-
-    loop(1, 11, unpack)
+    def unpack(q, rows):
+        for r, n in rows:
+            both = pk1[q, pl.ds(r, n), :]
+            g1[2 * q, pl.ds(r, n), :] = jnp.where(even[:n], both, roll(both, 1, 1))
+            g1[2 * q + 1, pl.ds(r, n), :] = jnp.where(even[:n], roll(both, -1, 1), both)
+
+    rim1 = [(8, 8), (48, 8)]
+    loop(1, 4, lambda q: unpack(q, all1))
+    loop(8, 11, lambda q: unpack(q, all1))
+    loop(4, 8, lambda q: unpack(q, rim1))
     v0_in = exchange(3, vb0, vs0, 3, 16, 3, 64, 3)
-    l1.first_sweep(g1, va1, (2, 22), all1)
+    l1.first_sweep(g1, va1, (2, 8), all1)
+    l1.first_sweep(g1, va1, (16, 22), all1)
+    l1.first_sweep(g1, va1, (8, 16), rim1)
     l1.sweep(va1, g1, vb1, (3, 21), all1)
     coarsen(
         functools.partial(l1.residual, vb1, g1), 2, tmp2, g2, (2, 10, lambda j: 2 * j), all1, 12
@@ -433,9 +440,8 @@
         yg[pl.ds(8 * (4 * parity + gy) + p, 1), :] = row
     yg_in = gather_near(yg, gather_sem.at[2], gather_sem.at[3])
     for x in range(4, 8):
-        w2[0, x, pl.ds(16, 16), :] = vb2[x, pl.ds(16, 16), :]
-        w2[1, x, pl.ds(16, 16), :] = g2[x, pl.ds(16, 16), :]
-    w2_in = exchange(4, w2, w2, 4, 4, 4, 16, 8)
+        pk2[x, pl.ds(16, 16), :] = jnp.where(even[:16], vb2[x, pl.ds(16, 16), :], g2[x, pl.ds(16, 16), :])
+    w2_in = exchange(4, pk2, pk2, 4, 4, 4, 16, 8)
     arrive(xk_in)
     shape = (SLOTS, LANES)
     pack3, pack4 = Packed3(shape), Packed4(shape)
@@ -485,7 +491,7 @@
         c = f4[5] * pack4.z_next([v])[0] + f4[6] * pack4.z_prev([v])[0]
         return ((1.0 - OMEGA) * v + start) + (a + b) + c
 
-    v4 = lax.fori_loop(0, 7, coarsest, start)
+    v4 = lax.fori_loop(0, 7, coarsest, start, unroll=7)
     v = []
     for i in range(4):
         y = l // 8 - 4 * i
@@ -515,11 +521,13 @@
     arrive(w2_in)
 
     def correct2(x):
-        va2[x, pl.ds(8, 32), :] = w2[0, x, pl.ds(8, 32), :] + dup2[x // 2]
+        both = pk2[x, pl.ds(8, 32), :]
+        va2[x, pl.ds(8, 32), :] = jnp.where(even[:32], both, roll(both, 1, 1)) + dup2[x // 2]
+        w2[x, pl.ds(8, 32), :] = jnp.where(even[:32], roll(both, -1, 1), both)
 
     loop(0, 12, correct2)
-    l2.sweep(va2, w2.at[1], vb2, (1, 11), all2)
-    l2.sweep(vb2, w2.at[1], va2, (2, 10), all2)
+    l2.sweep(va2, w2, vb2, (1, 11), all2)
+    l2.sweep(vb2, w2, va2, (2, 10), all2)
 
     def double2(x):
         c = va2[x, pl.ds(12, 24), :]
@@ -578,7 +586,7 @@
     n0, n1, n2 = (22, 96, LANES), (24, 64, LANES), (12, 48, LANES)
     scratch = [vmem(3, *n0)] + [vmem(*n0)] * 9 + [vmem(16, 64, LANES)]
     scratch += [vmem(*n1)] * 10 + [vmem(12, 64, LANES)] * 2
-    scratch += [vmem(*n2)] * 10 + [vmem(2, *n2), vmem(6, 32, LANES)]
+    scratch += [vmem(*n2)] * 10 + [vmem(*n2), vmem(*n2), vmem(6, 32, LANES)]
     scratch += [vmem(18, 96, LANES), vmem(12, 64, LANES), vmem(16, 96, LANES)]
     scratch += [vmem(64, LANES)] * 2 + [vmem(8 * SLOTS, LANES)] * 2
     scratch += [vmem(5, 8, SLOTS, LANES), vmem(7, SLOTS, LANES), vmem(8, SLOTS, LANES)]

time: 39.7 us -> 39.8 us (level)
  no operation moved by 1% of the time
where the time goes in v6:
time: 39.8 us; the launch traced here: 39.7 us
  Pallas kernels  37.5 us (94%)
  local copies, waits for them, and re-layouts  1.59 us (4%)
  between operations  0.64 us (2%)
    pallas_call x1, Pallas kernels, per_device(): pl.pallas_call(functools.partial(kernel, ngx, ngy), out_shape=(block, blo...  37.5 us
    unnamed x2, local copies, waits for them, and re-layouts  1.59 us

profile of v6, /device:TPU:1, one launch (start us, length us, event | category | flops | bytes accessed | tf_op | source)
XLA Modules:
  0.0 39.7 jit_solution(13432389243573999554)
XLA Ops:
  0.6 37.5 %shard_map.50 = (f32[16,64,128]{2,1,0:T(8,128)S(1)}, f32[16,64,128]{2,1,0:T(8,128)S(1)}) custom-call(f32[16,64,128]{2,1,0:T(8,128)} %p_hbm.1, f32[16,64,128]{2,1,0:T(8,128)} %k_hbm.1, f32[16,64,128]{2,1,0:T(8,128)} %s_hbm.1), custom_call_target="tpu_custom_call" | custom-call | tf_op jit(solution)/shard_map/pallas_call | solution.py:598
  38.1 0.8 %copy.7 = f32[16,64,128]{2,1,0:T(8,128)} copy(f32[16,64,128]{2,1,0:T(8,128)S(1)} %get-tuple-element.4) | data formatting | bytes 1048576
  38.9 0.8 %copy.8 = f32[16,64,128]{2,1,0:T(8,128)} copy(f32[16,64,128]{2,1,0:T(8,128)S(1)} %get-tuple-element.5) | data formatting | bytes 1048576
